TPU v7x, 32 devices: a whole 2x2x4 slice. The times are simulated.
32 devices in a mesh: leaf: 4 (over y, core), prow: 4 (over z), pcol: 2 (over x).
Axes of the slice: x: 2, y: 2, z: 4, core: 2. Of those that a mesh axis runs over, the one named last changes fastest.
Arguments:
- front_pivot: float32 [4, 1536, 1536], P('leaf', ('prow', 'pcol')), as said below
- front_lower: float32 [4, 6144, 1536], P('leaf', ('prow', 'pcol')), may hold values from -0.375 to 0.375
- front_rest: float32 [4, 6144, 6144], P('leaf', ('prow', 'pcol')), as said below
- parent_front: float32 [4, 8192, 4096], P('leaf', ('prow', 'pcol')), may hold values from -1.3 to 4.4, as said below
- relation: int32 [4, 6144], replicated, may hold values from 0 to 8191, as said below
Outputs:
- factor_pivot: float32 [4, 1536, 1536], P('leaf', ('prow', 'pcol'))
- factor_lower: float32 [4, 6144, 1536], P('leaf', ('prow', 'pcol'))
- parent_out: float32 [4, 8192, 4096], P('leaf', ('prow', 'pcol'))
Inputs may be any that keep to these rules, and one draw needn't show every extreme that they name: Each front_pivot[g] is symmetric positive definite, with no eigenvalue under 0.3. Each front_rest[g] is symmetric, with diagonal entries between 6 and 9 and small off-diagonal entries. `parent_front`: the two column halves of one parent front together form a symmetric matrix. `relation`: for every front and every k, the entries k * 768 to (k + 1) * 768 - 1 rise strictly and lie in k * 1024 to (k + 1) * 1024 - 1, and take both ends of that range.
All inputs are finite; a program needn't handle non-finite values.
Results may differ from a plain program's by a relative error of at most 0.0029.
Values may be sent and summed in bfloat16 or wider, within the bound.
No kernel may reach another device: no remote copies, remote signals or barrier semaphores. Data moves between devices by JAX's collectives and lax.ppermute only.
A program may use at most 192 MiB of HBM per device.

v0:
```python
import math

import jax
import jax.numpy as jnp
from jax import lax
from jax.experimental import pallas as pl
from jax.experimental.pallas import tpu as pltpu
from jax.sharding import PartitionSpec as P

ROWS = ("prow", "pcol")
bf16 = jnp.bfloat16
f32 = jnp.float32
LANES = 128
SUBS = 8
GROUP = 32
TALL = 768
VMEM_LIMIT = 56 << 20


def panel_widths(order):
    narrow = order // 6
    return (narrow, 2 * narrow, 2 * narrow, narrow)


def split(x):
    top = x.astype(bf16)
    return top, (x - top.astype(f32)).astype(bf16)


def left_parts(x):
    top, low = split(x)
    return jnp.concatenate([top, top, low], axis=1)


def right_parts(x):
    top, low = split(x)
    return jnp.concatenate([top, low, top], axis=1)


def nt(a, b):
    return lax.dot_general(a, b, (((1,), (1,)), ((), ())), preferred_element_type=f32)


def nn(a, b):
    return jnp.dot(a, b, preferred_element_type=f32)


def spread_lane(x, lane):
    return jnp.broadcast_to(x[:, lane:lane + 1], (SUBS, LANES))


def spread_sub(x, sub):
    return jnp.broadcast_to(x[sub:sub + 1, :], (SUBS, LANES))


def factor_square(square):
    lane = lax.broadcasted_iota(jnp.int32, (SUBS, LANES), 1)
    sub = lax.broadcasted_iota(jnp.int32, (SUBS, LANES), 0)
    count = LANES // SUBS
    span = GROUP // SUBS
    state = [square[SUBS * r:SUBS * (r + 1), :] for r in range(count)]
    inverses = []
    for b in range(count):
        first = SUBS * b
        last = (b // span + 1) * span
        block = state[b]
        inside = (lane >= first) & (lane < first + SUBS)
        columns = [spread_lane(block, first + k) for k in range(SUBS)]
        d = [
            [spread_sub(columns[k], i) if k >= i else None for k in range(SUBS)]
            for i in range(SUBS)
        ]
        packed = jnp.where(inside, (lane - first == sub).astype(f32), block)
        rows = [spread_sub(packed, i) for i in range(SUBS)]
        follow = b + 1 < last
        if follow:
            ahead = state[b + 1]
            beside = [spread_lane(ahead, first + k) for k in range(SUBS)]
            ahead = jnp.where(inside, 0.0, ahead)
        scales, steps = [], []
        for i in range(SUBS):
            scale = lax.rsqrt(d[i][i])
            scales.append(scale)
            step = [d[i][k] * scale if k > i else None for k in range(SUBS)]
            steps.append(step)
            rows[i] = rows[i] * scale
            for k in range(i + 1, SUBS):
                for m in range(k, SUBS):
                    d[k][m] = d[k][m] - step[k] * step[m]
            for k in range(i + 1, SUBS):
                rows[k] = rows[k] - step[k] * rows[i]
            if follow:
                beside[i] = beside[i] * scale
                ahead = ahead - beside[i] * rows[i]
                for k in range(i + 1, SUBS):
                    beside[k] = beside[k] - step[k] * beside[i]
        whole = rows[0]
        for i in range(1, SUBS):
            whole = jnp.where(sub == i, rows[i], whole)
        inverses.append(whole)
        if follow:
            state[b + 1] = ahead
        if b + 2 < last:
            back = [None] * SUBS
            for i in reversed(range(SUBS)):
                total = rows[i]
                for k in range(i + 1, SUBS):
                    total = total - steps[i][k] * back[k]
                back[i] = total * scales[i]
            for r in range(b + 2, last):
                below = state[r]
                left = [spread_lane(below, first + k) for k in range(SUBS)]
                below = jnp.where(inside, 0.0, below)
                for k in range(SUBS):
                    below = below - left[k] * back[k]
                state[r] = below
        if b + 1 == last and last < count:
            start = GROUP * (b // span)
            solved = jnp.concatenate(
                [
                    jnp.where((lane >= SUBS * (g + 1)) & (lane < SUBS * last), 0.0, inverses[g])
                    for g in range(b + 1 - span, b + 1)
                ],
                axis=0,
            )
            after = jnp.concatenate(state[last:], axis=0)
            own = slice(start, start + GROUP)
            left = nt(left_parts(after[:, own]), right_parts(solved[:, own]))
            top, low = split(solved)
            change = nn(left_parts(left), jnp.concatenate([top, low, top], axis=0))
            for r in range(last, count):
                at = SUBS * (r - last)
                done = (lane >= start) & (lane < start + GROUP)
                state[r] = jnp.where(done, 0.0, state[r]) - change[at:at + SUBS, :]
    return jnp.concatenate(
        [jnp.where(lane < SUBS * (b + 1), inverses[b], 0.0) for b in range(count)], axis=0
    )


def largest_tile(rows):
    return next(t for t in (256, 128, 64, 32, 16, 8) if rows % t == 0)


def tall_tile(rows):
    return next(rows // n for n in range(1, rows) if rows % n == 0 and rows // n <= TALL)


def panel_kernel(first, base, bases, pcols, turned, corner_at, *refs):
    refs = list(refs)
    place, shares, refs = refs[0], refs[1:1 + pcols], refs[1 + pcols:]
    before = len(bases)
    earlier = [(refs[2 * q], refs[2 * q + 1]) for q in range(before)]
    refs = refs[2 * before:]
    waits = len(refs) - 5 - before
    lower_in = refs[0]
    pivot, lower, rounded, side, tops = refs[waits:waits + 5]
    crowns = refs[waits + 5:]
    side[0] = place[2]
    width = pivot.shape[1]
    count = width // LANES
    skip = first - base
    bottom = skip + width
    for q in range(before):
        for t in range(count):
            at = first - bases[q] + t * LANES
            crowns[q][t * LANES:(t + 1) * LANES, :] = right_parts(
                earlier[q][0][at:at + LANES, :]
            )
    low, left = corner_at
    prows, share_rows = shares[0].shape[:2]
    for apart in range(pcols):
        source = lax.rem(place[1] - apart + pcols, pcols)
        for r in range(prows - low):
            line = lax.rem(place[0] - r + prows, prows) if turned else r
            at = pl.multiple_of((line * pcols + source) * share_rows, 8)
            pivot[pl.ds(at, share_rows), :] = shares[apart][low + r, :, left:left + width]
    pltpu.sync_copy(lower_in.at[:, first:first + width], lower)

    def subtract(target, pasts, offsets):
        tile = tall_tile(target.shape[0])

        @pl.loop(0, target.shape[0] // tile)
        def _(t):
            at = pl.multiple_of(t * tile, tile)
            values = target[pl.ds(at, tile), :]
            for q in range(before):
                past = pasts[q][pl.ds(pl.multiple_of(offsets[q] + at, 8), tile), :]
                values = values - nt(left_parts(past), crowns[q][...])
            target[pl.ds(at, tile), :] = values

    if before:
        subtract(pivot, [past for past, _ in earlier], [base - b for b in bases])
        subtract(lower, [past for _, past in earlier], [0] * before)
    if skip:
        pivot[0:skip, :] = jnp.zeros((skip, width), f32)

    row = lax.broadcasted_iota(jnp.int32, (width, LANES), 0)
    lane = lax.broadcasted_iota(jnp.int32, (width, LANES), 1)

    @pl.loop(0, count)
    def _(k):
        here = pl.ds(pl.multiple_of(k * LANES, LANES), LANES)
        corner = pl.ds(pl.multiple_of(skip + k * LANES, LANES), LANES)
        solver = right_parts(factor_square(pivot[corner, here]))
        solved = nt(left_parts(pivot[skip:bottom, here]), solver)
        solved = jnp.where(row - k * LANES >= lane, solved, 0.0)
        pivot[skip:bottom, here] = solved
        solved = jnp.where(row >= (k + 1) * LANES, solved, 0.0)
        tops[...] = right_parts(solved)
        if count > 1:
            pivot[skip:bottom, LANES:] -= nt(left_parts(solved), tops[LANES:, :])

        def run(ref, start, rows):
            tile = tall_tile(rows)

            @pl.loop(0, rows // tile)
            def _(t):
                band = pl.ds(pl.multiple_of(start + t * tile, 8), tile)
                solved = nt(left_parts(ref[band, here]), solver)
                ref[band, here] = solved
                if count > 1:
                    ref[band, LANES:] -= nt(left_parts(solved), tops[LANES:, :])

        if pivot.shape[0] > bottom:
            run(pivot, bottom, pivot.shape[0] - bottom)
        run(lower, 0, lower.shape[0])

    tile = largest_tile(lower.shape[0])

    @pl.loop(0, lower.shape[0] // tile)
    def _(t):
        here = pl.ds(pl.multiple_of(t * tile, tile), tile)
        rounded[here, :] = lower[here, :].astype(bf16)


def factor_panel(first, width, place, shares, turned, corner_at, lower, earlier, after):
    prows, share_rows, _ = shares[0].shape
    rows = len(shares) * (prows - corner_at[0]) * share_rows
    order = lower.shape[1]
    base = order - rows
    flat = [past for pair in earlier for past in pair]
    in_vmem = pl.BlockSpec(memory_space=pltpu.VMEM)
    anywhere = pl.BlockSpec(memory_space=pl.ANY)
    bases = [order - past.shape[0] for past, _ in earlier]
    return pl.pallas_call(
        lambda *refs: panel_kernel(first, base, bases, len(shares), turned, corner_at, *refs),
        out_shape=(
            jax.ShapeDtypeStruct((rows, width), f32),
            jax.ShapeDtypeStruct((lower.shape[0], width), f32),
            jax.ShapeDtypeStruct((lower.shape[0], width), bf16),
            jax.ShapeDtypeStruct((1,), jnp.int32),
        ),
        in_specs=[pl.BlockSpec(memory_space=pltpu.SMEM)]
        + [in_vmem] * (len(shares) + len(flat))
        + [anywhere] * (1 + len(after)),
        out_specs=[in_vmem] * 3 + [pl.BlockSpec(memory_space=pltpu.SMEM)],
        scratch_shapes=[pltpu.VMEM((width, 3 * LANES), bf16)]
        + [pltpu.VMEM((width, 3 * past.shape[1]), bf16) for past, _ in earlier],
        compiler_params=pltpu.CompilerParams(vmem_limit_bytes=VMEM_LIMIT),
        cost_estimate=pl.CostEstimate(
            flops=width * 50000000,
            bytes_accessed=10 * width * (rows + lower.shape[0]),
            transcendentals=0,
        ),
    )(place, *shares, *flat, lower, *after)


def one_hot(links, window):
    places = lax.broadcasted_iota(jnp.int32, (window, links.shape[1]), 0)
    return (places == links).astype(bf16)


def rest_kernel(whole, half, values, *refs):
    out, table, placed = refs[-3:]
    if whole:
        out, leaving = refs[-4:-2]
        leaving[...] = refs[0][...]
        refs = refs[1:]
    row_links, col_links, parent = refs[:3]
    window = out.shape[0]
    rows = values.shape[0]

    @pl.when(pl.program_id(0) == 0)
    def _():
        spread = one_hot(row_links[0], window)
        table[:, :rows] = spread
        table[:, rows:] = spread

    tile = largest_tile(out.shape[1])
    count = col_links.shape[0]
    step = pl.program_id(0)
    mine = (half[1] >= step * count) & (half[1] < (step + 1) * count)

    def spread_of(part, at, depth):
        for i in range(count):
            spread = one_hot(col_links[i, 0], window)
            block, area = slice(i * rows, (i + 1) * rows), slice(i * window, (i + 1) * window)
            placed[at:at + rows, area] = nt(part[:, block], spread).astype(bf16)
        if depth:

            @pl.loop(0, out.shape[1] // tile)
            def _(t):
                here = pl.ds(pl.multiple_of(t * tile, tile), tile)
                out[:, here] = parent[:, here] + nn(table[:, :depth], placed[:depth, here])

    @pl.when(mine)
    def _():
        top, low = split(values[...])
        spread_of(top, 0, 0)
        spread_of(low, rows, 2 * rows)

    @pl.when(jnp.logical_not(mine))
    def _():
        spread_of(values[...].astype(bf16), 0, rows)


def add_rest(parent, values, half, row_links, col_links, after, whole):
    window = parent.shape[0]
    rows = values.shape[0]
    group = LANES // math.gcd(LANES, rows)
    steps = parent.shape[1] // window // group
    area = pl.BlockSpec((window, group * window), lambda w, half: (0, w))
    block = (rows, group * rows)
    total = jax.ShapeDtypeStruct(parent.shape, f32)
    crossing = [pl.BlockSpec(block, lambda w, half: (0, (1 - half[0]) * steps + w))]
    leaving = pl.BlockSpec(block, lambda w, half: (0, w))
    return pl.pallas_call(
        lambda *refs: rest_kernel(whole, *refs),
        out_shape=(total, jax.ShapeDtypeStruct((rows, values.shape[1] // 2), f32)) if whole else total,
        grid_spec=pltpu.PrefetchScalarGridSpec(
            num_scalar_prefetch=1,
            grid=(steps,),
            in_specs=[pl.BlockSpec(block, lambda w, half: (0, half[0] * steps + w))]
            + (crossing if whole else [])
            + [
                pl.BlockSpec((1, 1, rows), lambda w, half: (0, 0, 0)),
                pl.BlockSpec((group, 1, 1, rows), lambda w, half: (w, 0, 0, 0)),
                area,
            ]
            + [pl.BlockSpec(memory_space=pl.ANY)] * len(after),
            out_specs=(area, leaving) if whole else area,
            scratch_shapes=[
                pltpu.VMEM((window, 2 * rows), bf16),
                pltpu.VMEM((2 * rows, group * window), bf16),
            ],
        ),
        input_output_aliases={} if whole else {4: 0},
        compiler_params=pltpu.CompilerParams(vmem_limit_bytes=VMEM_LIMIT),
        cost_estimate=pl.CostEstimate(
            flops=4 * rows * parent.size + 4 * rows * rows * parent.shape[1],
            bytes_accessed=8 * parent.size + 4 * rows * rows * steps * group,
            transcendentals=0,
        ),
    )(
        half,
        *([values] * (2 if whole else 1)),
        row_links,
        col_links,
        parent,
        *after,
    )


def rows_kernel(own, other, own_links, other_links, out):
    window, width = out.shape[0], own.shape[1]
    for source, (values, links) in enumerate(((own, own_links), (other, other_links))):
        out[:, source * width:(source + 1) * width] = nn(
            one_hot(links[0], window), values[...]
        ).astype(bf16)


def spread_rows(own, other, row_links, window):
    return pl.pallas_call(
        rows_kernel,
        out_shape=jax.ShapeDtypeStruct((window, 2 * own.shape[1]), bf16),
        compiler_params=pltpu.CompilerParams(vmem_limit_bytes=VMEM_LIMIT),
        cost_estimate=pl.CostEstimate(
            flops=4 * window * own.size, bytes_accessed=12 * own.size, transcendentals=0
        ),
    )(own, other, *row_links)


def update_kernel(places, rows, own, other, own_links, other_links, total, *refs):
    out, cols = refs[-2:]
    window, width = cols.shape[0], own.shape[2]

    @pl.when(pl.program_id(1) == 0)
    def _():
        for source, (values, links) in enumerate(((own, own_links), (other, other_links))):
            cols[:, source * width:(source + 1) * width] = nn(
                one_hot(links[0, 0], window), values[0]
            ).astype(bf16)

    tile = out.shape[1]
    here = pl.ds(pl.multiple_of(pl.program_id(1) * tile, tile), tile)
    out[...] = total[...] - nt(rows[...], cols[here, :])


def update_windows(total, rows, own, other, places, col_links, after):
    window = total.shape[0]
    count, children, width = own.shape
    tile = largest_tile(window)
    block = pl.BlockSpec((1, children, width), lambda i, t, places: (i, 0, 0))
    link = pl.BlockSpec((1, 1, 1, children), lambda i, t, places: (places[i], 0, 0, 0))
    area = pl.BlockSpec(
        (window, tile), lambda i, t, places: (0, places[i] * (window // tile) + t)
    )
    return pl.pallas_call(
        update_kernel,
        out_shape=jax.ShapeDtypeStruct(total.shape, f32),
        grid_spec=pltpu.PrefetchScalarGridSpec(
            num_scalar_prefetch=1,
            grid=(count, window // tile),
            in_specs=[
                pl.BlockSpec((window, 2 * width), lambda i, t, places: (0, 0)),
                block,
                block,
                link,
                link,
                area,
            ]
            + [pl.BlockSpec(memory_space=pl.ANY)] * len(after),
            out_specs=area,
            scratch_shapes=[pltpu.VMEM((window, 2 * width), bf16)],
        ),
        input_output_aliases={6: 0},
        compiler_params=pltpu.CompilerParams(vmem_limit_bytes=VMEM_LIMIT),
        cost_estimate=pl.CostEstimate(
            flops=4 * count * window * width * (window + children),
            bytes_accessed=8 * count * window * window,
            transcendentals=0,
        ),
    )(places, rows, own, other, *col_links, total, *after)


def local(front_pivot, front_lower, front_rest, parent_front, relation):
    leaves, prows, pcols = (lax.axis_size(a) for a in ("leaf", "prow", "pcol"))
    position = lax.axis_index(ROWS)
    across = lax.axis_index("pcol")
    pivot_rows, lower_rows = front_pivot[0], front_lower[0]
    rest_rows, parent_rows = front_rest[0], parent_front[0]
    rows_here, pivot_order = pivot_rows.shape
    block_rows, child_order = rest_rows.shape
    window = parent_rows.shape[0]
    child_half = child_order // 2
    blocks = child_half // block_rows
    near = prows // 2
    leaf_index = lax.axis_index("leaf")
    side = leaf_index % 2
    partner = leaf_index + 1 - 2 * side

    def to_sibling(value):
        return lax.ppermute(value, "leaf", [(g, g ^ 1) for g in range(leaves)])

    def to_cols(value, apart, swap):
        pairs = [
            ((g * prows + r) * pcols + c, ((g ^ swap) * prows + r) * pcols + (c + apart) % pcols)
            for g in range(leaves)
            for r in range(prows)
            for c in range(pcols)
        ]
        return lax.ppermute(value, ("leaf",) + ROWS, pairs)

    def links_of(child):
        links = lax.dynamic_index_in_dim(relation, child, 0, keepdims=False)
        rows = lax.dynamic_slice_in_dim(links, position * block_rows, block_rows, 0)
        cols = lax.dynamic_slice_in_dim(links, side * child_half, child_half, 0)
        cols = cols.reshape(blocks, 1, 1, block_rows)
        first = side * blocks + jnp.arange(blocks, dtype=jnp.int32)
        return (
            (rows - position * window).reshape(1, 1, block_rows),
            cols - first.reshape(blocks, 1, 1, 1) * window,
        )

    own_row_links, own_col_links = links_of(leaf_index)
    other_row_links, other_col_links = links_of(partner)
    row_links = (own_row_links, other_row_links)
    col_links = (own_col_links, other_col_links)

    widths = panel_widths(pivot_order)
    starts = [sum(widths[:p]) for p in range(len(widths))]
    def along(value, step):
        return lax.ppermute(value, "prow", [(r, (r + step) % prows) for r in range(prows)])

    across_z = rows_here * pcols
    column_blocks = []
    spans = [(starts[0], starts[1]), (starts[1], starts[2]), (starts[2], pivot_order)]
    for n, (s, end) in enumerate(spans):
        mine = pivot_rows[:, s:end]
        if n == 0:
            mine = jnp.stack([mine] + [along(mine, step) for step in range(1, prows)])
        else:
            mine = lax.all_gather(mine, "prow", axis=0)[s // across_z:]
        column_blocks.append([mine] + [to_cols(mine, apart, 0) for apart in range(1, pcols)])

    def update(total, p, before_first, before_last):
        rounded, other, owns, others = panels[p]
        rows = spread_rows(rounded, other, row_links, window)
        for apart in range(pcols):
            places = jnp.arange(near, dtype=jnp.int32) * pcols + lax.rem(
                across - apart + pcols, pcols
            ).astype(jnp.int32)
            total = update_windows(
                total,
                rows,
                owns[apart],
                others[apart],
                places,
                col_links,
                before_last if apart == pcols - 1 else () if apart else before_first,
            )
        return total

    own_block = (position - side * blocks).astype(jnp.int32)
    done, panels, lines = [], [], []
    place = jnp.stack([lax.axis_index("prow"), across, side]).astype(jnp.int32)

    def pass_on(p, side_now):
        rounded, other, line = lines[p]
        kept = lax.dynamic_slice_in_dim(line, side_now * near, near, 0)
        sent = lax.dynamic_slice_in_dim(line, (1 - side_now) * near, near, 0)
        owns = [to_cols(kept, apart, 0) if apart else kept for apart in range(pcols)]
        others = [to_cols(sent, apart, 1) for apart in range(pcols)]
        panels.append((rounded, other, owns, others))
        return (kept, sent), tuple(owns[1:] + others)

    parts = []
    for p, (s, w) in enumerate(zip(starts, widths)):
        n = min(p, len(spans) - 1)
        if p == 0:
            start_total, leaving = add_rest(
                parent_rows,
                rest_rows,
                jnp.stack([side.astype(jnp.int32), own_block]),
                own_row_links,
                own_col_links,
                (column_blocks[0][-1], column_blocks[1][0]),
                True,
            )
            waits = (start_total, column_blocks[2][0])
        elif p == 2:
            waits = parts[0][1]
        elif p == 3:
            total = add_rest(
                start_total,
                to_sibling(leaving),
                jnp.stack([jnp.zeros((), jnp.int32), own_block]),
                other_row_links,
                other_col_links,
                (),
                False,
            )
            total = update(total, 0, parts[1][0], ())
            waits = (total,)
        corner_at = (s // across_z - spans[n][0] // across_z, s - spans[n][0])
        pivot, lower, rounded, side_now = factor_panel(
            s, w, place, column_blocks[n], p == 0, corner_at, lower_rows, done, waits
        )
        done.append((pivot, lower))
        lines.append((rounded, to_sibling(rounded), lax.all_gather(rounded, "prow", axis=0)))
        if p:
            parts.append(pass_on(p - 1, side_now[0]))
    parts.append(pass_on(len(starts) - 1, side_now[0]))

    for p in range(1, len(starts)):
        total = update(total, p, parts[p][1] if p == 1 else (), ())

    factor_rows = jnp.concatenate(
        [
            lax.dynamic_slice_in_dim(
                jnp.concatenate([jnp.zeros((pivot_order - pivot.shape[0], w), f32), pivot], axis=0),
                position * rows_here,
                rows_here,
                0,
            )
            for s, w, (pivot, _) in zip(starts, widths, done)
        ],
        axis=1,
    )
    lower_out = jnp.concatenate([lower for _, lower in done], axis=1)
    return (factor_rows[None], lower_out[None], total[None])


def solution(mesh):
    whole = P("leaf", ROWS, None)
    return jax.shard_map(
        local,
        mesh=mesh,
        in_specs=(whole, whole, whole, whole, P()),
        out_specs=(whole, whole, whole),
        check_vma=False,
    )
```

profile of v0, /device:TPU:9, one launch (start us, length us, event | category | flops | bytes accessed | tf_op | source)
XLA Modules:
  0.0 501.7 jit_solution(17897017120480142719)
XLA Ops:
  15.9 13.6 %collective-permute-done.1 = f32[192,256]{1,0:T(8,128)S(1)} collective-permute-done((f32[192,256]{1,0:T(8,128)S(1)}, f32[192,256]{1,0:T(8,128)S(1)}, u32[]{:S(2)}, u32[]{:S(2)}) %collective-permute-start.1) | collective-permute-done | bytes 196640 | tf_op jit(solution)/shard_map/ppermute | solution.py:483
  29.5 14.4 %collective-permute-done = f32[192,256]{1,0:T(8,128)S(1)} collective-permute-done((f32[192,256]{1,0:T(8,128)S(1)}, f32[192,256]{1,0:T(8,128)S(1)}, u32[]{:S(2)}, u32[]{:S(2)}) %collective-permute-start) | collective-permute-done | bytes 196640 | tf_op jit(solution)/shard_map/ppermute | solution.py:483
  49.0 6.4 %all-gather.13.cloned.1.call-done = f32[768,512]{1,0:T(8,128)} async-done(((f32[192,512]{1,0:T(8,128)}), f32[768,512]{1,0:T(8,128)}) %all-gather.13.cloned.1.call-update) | async-done | bytes 1572880 | tf_op jit(solution)/shard_map/all_gather | solution.py:493
  58.7 28.1 %shard_map.76 = (f32[1024,4096]{1,0:T(8,128)}, f32[768,3072]{1,0:T(8,128)}) custom-call(s32[2]{0:T(128)} %pad_add_fusion.1.refs_0_, f32[768,6144]{1,0:T(8,128)} %bitcast.54, f32[768,6144]{1,0:T(8,128)} %bitcast.55, s32[1,1,768]{2,1,0:T(1,128)} %get-tuple-element.50.refs_3_.own_links, s32[4,1,1,768]{3,2,1,0:T(1,128)} %get-tuple-element.52.refs_4_.own_links, ...), custom_call_target="tpu_custom_call" | custom-call | flops 22548578304 | bytes 42991616 | tf_op jit(solution)/shard_map/pallas_call | solution.py:327
  86.9 14.3 %collective-permute-start.10 = (f32[768,3072]{1,0:T(8,128)}, f32[768,3072]{1,0:T(8,128)}, u32[]{:S(2)}, u32[]{:S(2)}) collective-permute-start(f32[768,3072]{1,0:T(8,128)} %get-tuple-element.29), channel_id=1, source_target_pairs={{0,8},{8,0},{16,24},{24,16},{1,9},{9,1},{17,25},{25,17},{2,10},{10... | collective-permute-start | bytes 28311560 | tf_op jit(solution)/shard_map/ppermute | solution.py:453
  101.7 6.5 %all-gather.15.cloned.1.call-done = f32[768,768]{1,0:T(8,128)} async-done(((f32[192,768]{1,0:T(8,128)}), f32[768,768]{1,0:T(8,128)}) %all-gather.15.cloned.1.call-update) | async-done | bytes 2359312 | tf_op jit(solution)/shard_map/all_gather | solution.py:493
  110.6 16.5 %shard_map.77 = (f32[1536,256]{1,0:T(8,128)}, f32[768,256]{1,0:T(8,128)}, bf16[768,256]{1,0:T(8,128)(2,1)}, s32[1]{0:T(128)}) custom-call(s32[3]{0:T(128)} %pad_add_fusion.refs_0_, f32[4,192,256]{2,1,0:T(8,128)} %copy-done.15, f32[4,192,256]{2,1,0:T(8,128)} %copy-done.21, f32[768,1536]{1,0:T(8,128)} %bitcast.57, ...), custom_call_target="tpu_custom_call" | custom-call | flops 12800000000 | bytes 5898240 | tf_op jit(solution)/shard_map/pallas_call | solution.py:245
  127.1 12.0 %all-gather.19.cloned.1.call-start = ((), (), s32[]{:S(2)}) async-start(), calls=%async_computation.3 | async-start | bytes 3932160 | tf_op jit(solution)/shard_map/all_gather | solution.py:560
  140.3 34.0 %shard_map.78 = (f32[1536,512]{1,0:T(8,128)}, f32[768,512]{1,0:T(8,128)}, bf16[768,512]{1,0:T(8,128)(2,1)}, s32[1]{0:T(128)}) custom-call(s32[3]{0:T(128)} %pad_add_fusion.refs_0_, f32[4,192,512]{2,1,0:T(8,128)} %bitcast.63, f32[4,192,512]{2,1,0:T(8,128)} %copy-done.20, f32[1536,256]{1,0:T(8,128)} %get-tuple-element.21.refs_3_, ...), custom_call_target="tpu_custom_call" | custom-call | flops 25600000000 | bytes 11796480 | tf_op jit(solution)/shard_map/pallas_call | solution.py:245
  182.0 19.2 %collective-permute-done.5.refs_2_ = f32[2,192,768]{2,1,0:T(8,128)} collective-permute-done((f32[2,192,768]{2,1,0:T(8,128)S(1)}, f32[2,192,768]{2,1,0:T(8,128)}, u32[]{:S(2)}, u32[]{:S(2)}) %collective-permute-start.5) | collective-permute-done | bytes 1179680 | tf_op jit(solution)/shard_map/ppermute | solution.py:462
  201.2 3.2 collective-permute-start.9
  204.4 13.7 %collective-permute-done.6.refs_8_.own = bf16[2,768,256]{2,1,0:T(8,128)(2,1)} collective-permute-done((bf16[2,768,256]{2,1,0:T(8,128)(2,1)S(1)}, bf16[2,768,256]{2,1,0:T(8,128)(2,1)}, u32[]{:S(2)}, u32[]{:S(2)}) %collective-permute-start.6) | collective-permute-done | bytes 786464 | tf_op jit(solution)/shard_map/ppermute | solution.py:462
  218.1 3.2 collective-permute-start.19
  221.3 15.1 %collective-permute-done.8.refs_10_.other = bf16[2,768,256]{2,1,0:T(8,128)(2,1)} collective-permute-done((bf16[2,768,256]{2,1,0:T(8,128)(2,1)S(1)}, bf16[2,768,256]{2,1,0:T(8,128)(2,1)}, u32[]{:S(2)}, u32[]{:S(2)}) %collective-permute-start.8) | collective-permute-done | bytes 786464 | tf_op jit(solution)/shard_map/ppermute | solution.py:462
  236.3 35.1 %shard_map.79 = (f32[768,512]{1,0:T(8,128)}, f32[768,512]{1,0:T(8,128)}, bf16[768,512]{1,0:T(8,128)(2,1)}, s32[1]{0:T(128)}) custom-call(s32[3]{0:T(128)} %pad_add_fusion.refs_0_, f32[2,192,768]{2,1,0:T(8,128)} %bitcast.46, f32[2,192,768]{2,1,0:T(8,128)} %collective-permute-done.5.refs_2_, f32[1536,256]{1,0:T(8,128)} %get-tuple-element.21.refs_3_, ...), custom_call_target="tpu_custom_call" | custom-call | flops 25600000000 | bytes 7864320 | tf_op jit(solution)/shard_map/pallas_call | solution.py:245
  276.2 3.1 shard_map.80.rows
  279.3 4.7 shard_map.87.rows
  286.3 4.5 shard_map.86.rows
  290.8 3.4 constant_dynamic-slice_fusion.4
  296.0 22.6 %shard_map.81.total = f32[1024,4096]{1,0:T(8,128)} custom-call(s32[2]{0:T(128)} %pad_add_fusion.2.refs_0_, f32[768,3072]{1,0:T(8,128)} %collective-permute-done.10.refs_1_, s32[1,1,768]{2,1,0:T(1,128)} %get-tuple-element.49.other_links.refs_2_, s32[4,1,1,768]{3,2,1,0:T(1,128)} %get-tuple-element.51.refs_3_.other_links, ...), custom_call_target="tpu_custom_call", output_to_operand_aliasing={{}: (4, {})} | custom-call | flops 22548578304 | bytes 42991616 | tf_op jit(solution)/shard_map/pallas_call | solution.py:327
  318.6 14.1 %shard_map.82.total = f32[1024,4096]{1,0:T(8,128)} custom-call(s32[2]{0:T(128)} %fusion.places, bf16[1024,512]{1,0:T(8,128)(2,1)} %shard_map.80.rows, bf16[2,768,256]{2,1,0:T(8,128)(2,1)} %copy-done.2, bf16[2,768,256]{2,1,0:T(8,128)(2,1)} %collective-permute-done.7.refs_9_.other, ...), custom_call_target="tpu_custom_call", output_to_operand_aliasing={{}: (6, {})} | custom-call | flops 3758096384 | bytes 16777216 | tf_op jit(solution)/shard_map/pallas_call | solution.py:408
  332.7 14.0 %shard_map.83.refs_10_.total = f32[1024,4096]{1,0:T(8,128)} custom-call(s32[2]{0:T(128)} %fusion.1.places, bf16[1024,512]{1,0:T(8,128)(2,1)} %shard_map.80.rows, bf16[2,768,256]{2,1,0:T(8,128)(2,1)} %collective-permute-done.6.refs_8_.own, bf16[2,768,256]{2,1,0:T(8,128)(2,1)} %collective-permute-done.8.refs_10_.other, ...), custom_call_target="tpu_custom_call", output_to_operand_aliasing={{}: (6, {})} | custom-call | flops 3758096384 | bytes 16777216 | tf_op jit(solution)/shard_map/pallas_call | solution.py:408
  346.7 20.0 %shard_map.84 = (f32[384,256]{1,0:T(8,128)}, f32[768,256]{1,0:T(8,128)}, bf16[768,256]{1,0:T(8,128)(2,1)}, s32[1]{0:T(128)}) custom-call(s32[3]{0:T(128)} %pad_add_fusion.refs_0_, f32[2,192,768]{2,1,0:T(8,128)} %bitcast.47, f32[2,192,768]{2,1,0:T(8,128)} %collective-permute-done.5.refs_2_, f32[1536,256]{1,0:T(8,128)} %get-tuple-element.21.refs_3_, ...), custom_call_target="tpu_custom_call" | custom-call | flops 12800000000 | bytes 2949120 | tf_op jit(solution)/shard_map/pallas_call | solution.py:245
  368.0 3.5 collective-permute-start.11
  371.6 3.8 constant_dynamic-slice_fusion
  378.6 17.5 %shard_map.88.total = f32[1024,4096]{1,0:T(8,128)} custom-call(s32[2]{0:T(128)} %fusion.places, bf16[1024,1024]{1,0:T(8,128)(2,1)} %shard_map.87.rows, bf16[2,768,512]{2,1,0:T(8,128)(2,1)} %copy-done, bf16[2,768,512]{2,1,0:T(8,128)(2,1)} %copy-done.1, s32[4,1,1,768]{3,2,1,0:T(1,128)} %get-tuple-element.52.refs_4_.own_links, ...), custom_call_target="tpu_custom_call", output_to_operand_aliasing={{}: (6, {})} | custom-call | flops 7516192768 | bytes 16777216 | tf_op jit(solution)/shard_map/pallas_call | solution.py:408
  396.1 17.5 %shard_map.89.total = f32[1024,4096]{1,0:T(8,128)} custom-call(s32[2]{0:T(128)} %fusion.1.places, bf16[1024,1024]{1,0:T(8,128)(2,1)} %shard_map.87.rows, bf16[2,768,512]{2,1,0:T(8,128)(2,1)} %collective-permute-done.20.refs_0_.own, bf16[2,768,512]{2,1,0:T(8,128)(2,1)} %collective-permute-done.21.refs_2_.other, ...), custom_call_target="tpu_custom_call", output_to_operand_aliasing={{}: (6, {})} | custom-call | flops 7516192768 | bytes 16777216 | tf_op jit(solution)/shard_map/pallas_call | solution.py:408
  418.3 3.1 shard_map.85.rows
  423.3 17.3 %shard_map.90.total = f32[1024,4096]{1,0:T(8,128)} custom-call(s32[2]{0:T(128)} %fusion.places, bf16[1024,1024]{1,0:T(8,128)(2,1)} %shard_map.86.rows, bf16[2,768,512]{2,1,0:T(8,128)(2,1)} %get-tuple-element.38.own, bf16[2,768,512]{2,1,0:T(8,128)(2,1)} %collective-permute-done.18.other, ...), custom_call_target="tpu_custom_call", output_to_operand_aliasing={{}: (6, {})} | custom-call | flops 7516192768 | bytes 16777216 | tf_op jit(solution)/shard_map/pallas_call | solution.py:408
  446.2 17.5 %shard_map.91.total = f32[1024,4096]{1,0:T(8,128)} custom-call(s32[2]{0:T(128)} %fusion.1.places, bf16[1024,1024]{1,0:T(8,128)(2,1)} %shard_map.86.rows, bf16[2,768,512]{2,1,0:T(8,128)(2,1)} %copy-done.8, bf16[2,768,512]{2,1,0:T(8,128)(2,1)} %collective-permute-done.17.other, ...), custom_call_target="tpu_custom_call", output_to_operand_aliasing={{}: (6, {})} | custom-call | flops 7516192768 | bytes 16777216 | tf_op jit(solution)/shard_map/pallas_call | solution.py:408
  464.6 14.0 %shard_map.92.total = f32[1024,4096]{1,0:T(8,128)} custom-call(s32[2]{0:T(128)} %fusion.places, bf16[1024,512]{1,0:T(8,128)(2,1)} %shard_map.85.rows, bf16[2,768,256]{2,1,0:T(8,128)(2,1)} %copy-done.3, bf16[2,768,256]{2,1,0:T(8,128)(2,1)} %copy-done.18, s32[4,1,1,768]{3,2,1,0:T(1,128)} %get-tuple-element.52.refs_4_.own_links, ...), custom_call_target="tpu_custom_call", output_to_operand_aliasing={{}: (6, {})} | custom-call | flops 3758096384 | bytes 16777216 | tf_op jit(solution)/shard_map/pallas_call | solution.py:408
  480.6 14.0 %shard_map.93 = f32[1024,4096]{1,0:T(8,128)} custom-call(s32[2]{0:T(128)} %fusion.1.places, bf16[1024,512]{1,0:T(8,128)(2,1)} %shard_map.85.rows, bf16[2,768,256]{2,1,0:T(8,128)(2,1)} %copy-done.17, bf16[2,768,256]{2,1,0:T(8,128)(2,1)} %copy-done.16, s32[4,1,1,768]{3,2,1,0:T(1,128)} %get-tuple-element.52.refs_4_.own_links, ...), custom_call_target="tpu_custom_call", output_to_operand_aliasing={{}: (6, {})} | custom-call | flops 3758096384 | bytes 16777216 | tf_op jit(solution)/shard_map/pallas_call | solution.py:408
  (120 shorter events, 53.1 us)
Async XLA Ops:
  7.2 48.2 %all-gather.13.cloned.1.call-start = ((), (), s32[]{:S(2)}) async-start(), calls=%async_computation | async-start | bytes 1966080 | tf_op jit(solution)/shard_map/all_gather | solution.py:493
  9.1 99.1 %all-gather.15.cloned.1.call-start = ((), (), s32[]{:S(2)}) async-start(), calls=%async_computation.1 | async-start | bytes 2949120 | tf_op jit(solution)/shard_map/all_gather | solution.py:493
  10.0 167.0 %all-gather.17.cloned.1.call-start = ((), (), s32[]{:S(2)}) async-start(), calls=%async_computation.2 | async-start | bytes 1966080 | tf_op jit(solution)/shard_map/all_gather | solution.py:560
  10.1 5.8 %collective-permute-start.2 = (f32[192,256]{1,0:T(8,128)S(1)}, f32[192,256]{1,0:T(8,128)S(1)}, u32[]{:S(2)}, u32[]{:S(2)}) collective-permute-start(f32[192,256]{1,0:T(8,128)S(1)} %get-tuple-element.46), channel_id=1, source_target_pairs={{0,6},{2,0},{4,2},{6,4},{1,7},{3,1},{5,3},{7,5},{8,14},{10,8},{12,... | collective-permute-start | bytes 589832 | tf_op jit(solution)/shard_map/ppermute | solution.py:483
  10.2 19.4 %collective-permute-start.1 = (f32[192,256]{1,0:T(8,128)S(1)}, f32[192,256]{1,0:T(8,128)S(1)}, u32[]{:S(2)}, u32[]{:S(2)}) collective-permute-start(f32[192,256]{1,0:T(8,128)S(1)} %get-tuple-element.46), channel_id=1, source_target_pairs={{0,4},{2,6},{4,0},{6,2},{1,5},{3,7},{5,1},{7,3},{8,12},{10,14},{12... | collective-permute-start | bytes 589832 | tf_op jit(solution)/shard_map/ppermute | solution.py:483
  12.7 31.3 %collective-permute-start = (f32[192,256]{1,0:T(8,128)S(1)}, f32[192,256]{1,0:T(8,128)S(1)}, u32[]{:S(2)}, u32[]{:S(2)}) collective-permute-start(f32[192,256]{1,0:T(8,128)S(1)} %get-tuple-element.46), channel_id=1, source_target_pairs={{0,2},{2,4},{4,6},{6,0},{1,3},{3,5},{5,7},{7,1},{8,10},{10,12},{12... | collective-permute-start | bytes 589832 | tf_op jit(solution)/shard_map/ppermute | solution.py:483
  44.0 42.8 %copy-start.15 = (f32[4,192,256]{2,1,0:T(8,128)}, f32[4,192,256]{2,1,0:T(8,128)S(1)}, u32[]{:S(2)}) copy-start(f32[4,192,256]{2,1,0:T(8,128)S(1)} %pad_maximum_fusion.refs_1_) | copy-start | bytes 2359300
  44.0 13.8 %collective-permute-start.3 = (f32[4,192,256]{2,1,0:T(8,128)S(1)}, f32[4,192,256]{2,1,0:T(8,128)S(1)}, u32[]{:S(2)}, u32[]{:S(2)}) collective-permute-start(f32[4,192,256]{2,1,0:T(8,128)S(1)} %pad_maximum_fusion.refs_1_), channel_id=1, source_target_pairs={{0,1},{1,0},{2,3},{3,2},{4,5},{5,4},{6,7},{7,6},{8,9},{9,8},{10,11... | collective-permute-start | bytes 2359304 | tf_op jit(solution)/shard_map/ppermute | solution.py:462
  55.4 83.6 %collective-permute-start.4 = (f32[4,192,512]{2,1,0:T(8,128)}, f32[4,192,512]{2,1,0:T(8,128)S(1)}, u32[]{:S(2)}, u32[]{:S(2)}) collective-permute-start(f32[4,192,512]{2,1,0:T(8,128)} %bitcast.61), channel_id=1, source_target_pairs={{0,1},{1,0},{2,3},{3,2},{4,5},{5,4},{6,7},{7,6},{8,9},{9,8},{10,11... | collective-permute-start | bytes 4718600 | tf_op jit(solution)/shard_map/ppermute | solution.py:462
  86.9 209.1 %collective-permute-start.10 = (f32[768,3072]{1,0:T(8,128)}, f32[768,3072]{1,0:T(8,128)}, u32[]{:S(2)}, u32[]{:S(2)}) collective-permute-start(f32[768,3072]{1,0:T(8,128)} %get-tuple-element.29), channel_id=1, source_target_pairs={{0,8},{8,0},{16,24},{24,16},{1,9},{9,1},{17,25},{25,17},{2,10},{10... | collective-permute-start | bytes 28311560 | tf_op jit(solution)/shard_map/ppermute | solution.py:453
  127.1 163.7 %all-gather.19.cloned.1.call-start = ((), (), s32[]{:S(2)}) async-start(), calls=%async_computation.3 | async-start | bytes 3932160 | tf_op jit(solution)/shard_map/all_gather | solution.py:560
  174.4 197.2 %all-gather.23.cloned.1.call-start = ((), (), s32[]{:S(2)}) async-start(), calls=%async_computation.5 | async-start | bytes 3932160 | tf_op jit(solution)/shard_map/all_gather | solution.py:560
  174.4 26.8 %collective-permute-start.5 = (f32[2,192,768]{2,1,0:T(8,128)S(1)}, f32[2,192,768]{2,1,0:T(8,128)}, u32[]{:S(2)}, u32[]{:S(2)}) collective-permute-start(f32[2,192,768]{2,1,0:T(8,128)S(1)} %bitcast.48), channel_id=1, source_target_pairs={{0,1},{1,0},{2,3},{3,2},{4,5},{5,4},{6,7},{7,6},{8,9},{9,8},{10,11... | collective-permute-start | bytes 3538952 | tf_op jit(solution)/shard_map/ppermute | solution.py:462
  177.0 41.1 %copy-start.14 = (bf16[768,512]{1,0:T(8,128)(2,1)S(1)}, bf16[768,512]{1,0:T(8,128)(2,1)}, u32[]{:S(2)}) copy-start(bf16[768,512]{1,0:T(8,128)(2,1)} %get-tuple-element.30.own) | copy-start | bytes 2359300
  178.6 92.8 %copy-start.2 = (bf16[2,768,256]{2,1,0:T(8,128)(2,1)}, bf16[2,768,256]{2,1,0:T(8,128)(2,1)S(1)}, u32[]{:S(2)}) copy-start(bf16[2,768,256]{2,1,0:T(8,128)(2,1)S(1)} %get-tuple-element.44.own) | copy-start | bytes 2359300
  178.6 39.5 %collective-permute-start.6 = (bf16[2,768,256]{2,1,0:T(8,128)(2,1)S(1)}, bf16[2,768,256]{2,1,0:T(8,128)(2,1)}, u32[]{:S(2)}, u32[]{:S(2)}) collective-permute-start(bf16[2,768,256]{2,1,0:T(8,128)(2,1)S(1)} %get-tuple-element.44.own), channel_id=1, source_target_pairs={{0,1},{1,0},{2,3},{3,2},{4,5},{5,4},{6,7},{7,6},{8,9},{9,8},{10,11... | collective-permute-start | bytes 2359304 | tf_op jit(solution)/shard_map/ppermute | solution.py:462
  178.9 42.3 %collective-permute-start.7 = (bf16[2,768,256]{2,1,0:T(8,128)(2,1)S(1)}, bf16[2,768,256]{2,1,0:T(8,128)(2,1)}, u32[]{:S(2)}, u32[]{:S(2)}) collective-permute-start(bf16[2,768,256]{2,1,0:T(8,128)(2,1)S(1)} %get-tuple-element.43), channel_id=1, source_target_pairs={{0,8},{1,9},{2,10},{3,11},{4,12},{5,13},{6,14},{7,15},{8,0},{9,1},... | collective-permute-start | bytes 2359304 | tf_op jit(solution)/shard_map/ppermute | solution.py:462
  180.4 55.9 %collective-permute-start.8 = (bf16[2,768,256]{2,1,0:T(8,128)(2,1)S(1)}, bf16[2,768,256]{2,1,0:T(8,128)(2,1)}, u32[]{:S(2)}, u32[]{:S(2)}) collective-permute-start(bf16[2,768,256]{2,1,0:T(8,128)(2,1)S(1)} %get-tuple-element.43), channel_id=1, source_target_pairs={{0,9},{1,8},{2,11},{3,10},{4,13},{5,12},{6,15},{7,14},{8,1},{9,0},... | collective-permute-start | bytes 2359304 | tf_op jit(solution)/shard_map/ppermute | solution.py:462
  201.2 74.3 %collective-permute-start.9 = (bf16[768,256]{1,0:T(8,128)(2,1)}, bf16[768,256]{1,0:T(8,128)(2,1)S(1)}, u32[]{:S(2)}, u32[]{:S(2)}) collective-permute-start(bf16[768,256]{1,0:T(8,128)(2,1)} %get-tuple-element.25.own), channel_id=1, source_target_pairs={{0,8},{8,0},{16,24},{24,16},{1,9},{9,1},{17,25},{25,17},{2,10},{10... | collective-permute-start | bytes 1179656 | tf_op jit(solution)/shard_map/ppermute | solution.py:453
  218.1 61.3 %collective-permute-start.19 = (bf16[768,512]{1,0:T(8,128)(2,1)S(1)}, bf16[768,512]{1,0:T(8,128)(2,1)}, u32[]{:S(2)}, u32[]{:S(2)}) collective-permute-start(bf16[768,512]{1,0:T(8,128)(2,1)S(1)} %copy-done.14), channel_id=1, source_target_pairs={{0,8},{8,0},{16,24},{24,16},{1,9},{9,1},{17,25},{25,17},{2,10},{10... | collective-permute-start | bytes 2359304 | tf_op jit(solution)/shard_map/ppermute | solution.py:453
  271.4 14.9 %collective-permute-start.15 = (bf16[768,512]{1,0:T(8,128)(2,1)}, bf16[768,512]{1,0:T(8,128)(2,1)}, u32[]{:S(2)}, u32[]{:S(2)}) collective-permute-start(bf16[768,512]{1,0:T(8,128)(2,1)} %get-tuple-element.36.own), channel_id=1, source_target_pairs={{0,8},{8,0},{16,24},{24,16},{1,9},{9,1},{17,25},{25,17},{2,10},{10... | collective-permute-start | bytes 2359304 | tf_op jit(solution)/shard_map/ppermute | solution.py:453
  274.4 147.0 %all-gather.21.cloned.1.call-start = ((), (), s32[]{:S(2)}) async-start(), calls=%async_computation.4 | async-start | bytes 1966080 | tf_op jit(solution)/shard_map/all_gather | solution.py:560
  294.1 83.1 %collective-permute-start.21 = (bf16[2,768,512]{2,1,0:T(8,128)(2,1)}, bf16[2,768,512]{2,1,0:T(8,128)(2,1)}, u32[]{:S(2)}, u32[]{:S(2)}) collective-permute-start(bf16[2,768,512]{2,1,0:T(8,128)(2,1)} %get-tuple-element.39.refs_1_), channel_id=1, source_target_pairs={{0,9},{1,8},{2,11},{3,10},{4,13},{5,12},{6,15},{7,14},{8,1},{9,0},... | collective-permute-start | bytes 4718600 | tf_op jit(solution)/shard_map/ppermute | solution.py:462
  295.7 81.7 %collective-permute-start.22 = (bf16[2,768,512]{2,1,0:T(8,128)(2,1)}, bf16[2,768,512]{2,1,0:T(8,128)(2,1)S(1)}, u32[]{:S(2)}, u32[]{:S(2)}) collective-permute-start(bf16[2,768,512]{2,1,0:T(8,128)(2,1)} %get-tuple-element.39.refs_1_), channel_id=1, source_target_pairs={{0,8},{1,9},{2,10},{3,11},{4,12},{5,13},{6,14},{7,15},{8,0},{9,1},... | collective-permute-start | bytes 4718600 | tf_op jit(solution)/shard_map/ppermute | solution.py:462
  295.7 80.9 %collective-permute-start.20 = (bf16[2,768,512]{2,1,0:T(8,128)(2,1)S(1)}, bf16[2,768,512]{2,1,0:T(8,128)(2,1)}, u32[]{:S(2)}, u32[]{:S(2)}) collective-permute-start(bf16[2,768,512]{2,1,0:T(8,128)(2,1)S(1)} %get-tuple-element.40.refs_0_.own), channel_id=1, source_target_pairs={{0,1},{1,0},{2,3},{3,2},{4,5},{5,4},{6,7},{7,6},{8,9},{9,8},{10,11... | collective-permute-start | bytes 4718600 | tf_op jit(solution)/shard_map/ppermute | solution.py:462
  368.0 50.3 %collective-permute-start.11 = (bf16[768,256]{1,0:T(8,128)(2,1)}, bf16[768,256]{1,0:T(8,128)(2,1)}, u32[]{:S(2)}, u32[]{:S(2)}) collective-permute-start(bf16[768,256]{1,0:T(8,128)(2,1)} %get-tuple-element.34.own), channel_id=1, source_target_pairs={{0,8},{8,0},{16,24},{24,16},{1,9},{9,1},{17,25},{25,17},{2,10},{10... | collective-permute-start | bytes 1179656 | tf_op jit(solution)/shard_map/ppermute | solution.py:453
  375.4 69.6 %collective-permute-start.17 = (bf16[2,768,512]{2,1,0:T(8,128)(2,1)}, bf16[2,768,512]{2,1,0:T(8,128)(2,1)}, u32[]{:S(2)}, u32[]{:S(2)}) collective-permute-start(bf16[2,768,512]{2,1,0:T(8,128)(2,1)} %get-tuple-element.37), channel_id=1, source_target_pairs={{0,9},{1,8},{2,11},{3,10},{4,13},{5,12},{6,15},{7,14},{8,1},{9,0},... | collective-permute-start | bytes 4718600 | tf_op jit(solution)/shard_map/ppermute | solution.py:462
  376.7 46.7 %collective-permute-start.18 = (bf16[2,768,512]{2,1,0:T(8,128)(2,1)}, bf16[2,768,512]{2,1,0:T(8,128)(2,1)}, u32[]{:S(2)}, u32[]{:S(2)}) collective-permute-start(bf16[2,768,512]{2,1,0:T(8,128)(2,1)} %get-tuple-element.37), channel_id=1, source_target_pairs={{0,8},{1,9},{2,10},{3,11},{4,12},{5,13},{6,14},{7,15},{8,0},{9,1},... | collective-permute-start | bytes 4718600 | tf_op jit(solution)/shard_map/ppermute | solution.py:462
  377.2 67.8 %collective-permute-start.16 = (bf16[2,768,512]{2,1,0:T(8,128)(2,1)}, bf16[2,768,512]{2,1,0:T(8,128)(2,1)S(1)}, u32[]{:S(2)}, u32[]{:S(2)}) collective-permute-start(bf16[2,768,512]{2,1,0:T(8,128)(2,1)} %get-tuple-element.38.own), channel_id=1, source_target_pairs={{0,1},{1,0},{2,3},{3,2},{4,5},{5,4},{6,7},{7,6},{8,9},{9,8},{10,11... | collective-permute-start | bytes 4718600 | tf_op jit(solution)/shard_map/ppermute | solution.py:462
  422.9 40.8 %collective-permute-start.14 = (bf16[2,768,256]{2,1,0:T(8,128)(2,1)S(1)}, bf16[2,768,256]{2,1,0:T(8,128)(2,1)S(1)}, u32[]{:S(2)}, u32[]{:S(2)}) collective-permute-start(bf16[2,768,256]{2,1,0:T(8,128)(2,1)S(1)} %get-tuple-element.41), channel_id=1, source_target_pairs={{0,8},{1,9},{2,10},{3,11},{4,12},{5,13},{6,14},{7,15},{8,0},{9,1},... | collective-permute-start | bytes 2359304 | tf_op jit(solution)/shard_map/ppermute | solution.py:462
  440.6 38.1 %collective-permute-start.13 = (bf16[2,768,256]{2,1,0:T(8,128)(2,1)S(1)}, bf16[2,768,256]{2,1,0:T(8,128)(2,1)S(1)}, u32[]{:S(2)}, u32[]{:S(2)}) collective-permute-start(bf16[2,768,256]{2,1,0:T(8,128)(2,1)S(1)} %get-tuple-element.41), channel_id=1, source_target_pairs={{0,9},{1,8},{2,11},{3,10},{4,13},{5,12},{6,15},{7,14},{8,1},{9,0},... | collective-permute-start | bytes 2359304 | tf_op jit(solution)/shard_map/ppermute | solution.py:462
  442.0 36.7 %collective-permute-start.12 = (bf16[2,768,256]{2,1,0:T(8,128)(2,1)S(1)}, bf16[2,768,256]{2,1,0:T(8,128)(2,1)S(1)}, u32[]{:S(2)}, u32[]{:S(2)}) collective-permute-start(bf16[2,768,256]{2,1,0:T(8,128)(2,1)S(1)} %get-tuple-element.42.own), channel_id=1, source_target_pairs={{0,1},{1,0},{2,3},{3,2},{4,5},{5,4},{6,7},{7,6},{8,9},{9,8},{10,11... | collective-permute-start | bytes 2359304 | tf_op jit(solution)/shard_map/ppermute | solution.py:462
  (20 other events, 175.1 us)
Sparse Core Ops, SparseCore 0:
  10.1 45.2 all-gather.12
  57.6 50.6 all-gather.14
  127.2 36.4 all-gather.16
  174.5 61.6 all-gather.18
  274.5 61.6 all-gather.22
  371.7 35.6 all-gather.20
where the time goes:
time: 509 us; the launch traced here: 502 us
  Pallas kernels  298 us (59%)
  waiting for transfers between devices  94.2 us (19%)
  starting transfers between devices  53.5 us (11%)
  local copies, waits for them, and re-layouts  28.6 us (6%)
  between operations  18.7 us (4%)
  other arithmetic  8.92 us (2%)
    pallas_call x8, Pallas kernels, update_windows(): pl.pallas_call(update_kernel, out_shape=jax.ShapeDtypeStruct(total.shape,...  126 us
    pallas_call x4, Pallas kernels, factor_panel(): pl.pallas_call(lambda *refs: panel_kernel(first, base, bases, len(shares)...  106 us
    ppermute x15, waiting for transfers between devices, to_cols(): return lax.ppermute(value, ('leaf',) + ROWS, pairs)  52 us
    pallas_call x2, Pallas kernels, add_rest(): pl.pallas_call(lambda *refs: rest_kernel(whole, *refs), out_shape=(total,...  50.7 us
    ppermute x3, waiting for transfers between devices, along(): lax.ppermute(value, 'prow', [(r, (r + step) % prows) for r in range(prows)])  29.1 us
    ppermute x5, starting transfers between devices, to_sibling(): return lax.ppermute(value, 'leaf', [(g, g ^ 1) for g in range(leaves)])  24.2 us
    pallas_call x4, Pallas kernels, spread_rows(): pl.pallas_call(rows_kernel, out_shape=jax.ShapeDtypeStruct((window, 2 * o...  15.4 us
    all_gather x2, waiting for transfers between devices, local(): mine = lax.all_gather(mine, 'prow', axis=0)[s // across_z:]  12.9 us
  transfers between devices with their start and end apart: 29, of which 11 were waited for; matrix products, arithmetic and copies ran while one was open for 5% of the time, Pallas kernels for 57%

commit v1 on v0

--- a/solution.py
+++ b/solution.py
@@ -528,18 +528,18 @@
     for p, (s, w) in enumerate(zip(starts, widths)):
         n = min(p, len(spans) - 1)
         if p == 0:
+            waits = tuple(column_blocks[1]) + (column_blocks[2][0],)
+        elif p == 1:
             start_total, leaving = add_rest(
                 parent_rows,
                 rest_rows,
                 jnp.stack([side.astype(jnp.int32), own_block]),
                 own_row_links,
                 own_col_links,
-                (column_blocks[0][-1], column_blocks[1][0]),
+                (done[0][0],),
                 True,
             )
-            waits = (start_total, column_blocks[2][0])
-        elif p == 2:
-            waits = parts[0][1]
+            waits = (start_total,)
         elif p == 3:
             total = add_rest(
                 start_total,

time: 509 us -> 528 us (1.037)
  waiting for transfers between devices: 94.2 us -> 131 us
  starting transfers between devices: 53.5 us -> 31.9 us
    all_gather x2, waiting for transfers between devices: 12.9 us -> 54.5 us  [local(): mine = lax.all_gather(mine, 'prow', axis=0)[s // across_z:]]
    ppermute x5, starting transfers between devices: 24.2 us -> 5.27 us  [to_sibling(): return lax.ppermute(value, 'leaf', [(g, g ^ 1) for g in range(leaves)])]
    ppermute x15, waiting for transfers between devices: 52 us -> 45.3 us  [to_cols(): return lax.ppermute(value, ('leaf',) + ROWS, pairs)]
  transfers between devices with their start and end apart: 29 -> 29, of which waited for: 11 -> 8; matrix products, arithmetic and copies ran while one was open for 5% -> 5% of each run, Pallas kernels for 57% -> 46%
where the time goes in v1:
time: 528 us; the launch traced here: 520 us
  Pallas kernels  297 us (56%)
  waiting for transfers between devices  131 us (25%)
  starting transfers between devices  31.9 us (6%)
  local copies, waits for them, and re-layouts  31.2 us (6%)
  between operations  18.4 us (3%)
  other arithmetic  9.08 us (2%)
    pallas_call x8, Pallas kernels, update_windows(): pl.pallas_call(update_kernel, out_shape=jax.ShapeDtypeStruct(total.shape,...  126 us
    pallas_call x4, Pallas kernels, factor_panel(): pl.pallas_call(lambda *refs: panel_kernel(first, base, bases, len(shares)...  106 us
    all_gather x2, waiting for transfers between devices, local(): mine = lax.all_gather(mine, 'prow', axis=0)[s // across_z:]  54.5 us
    pallas_call x2, Pallas kernels, add_rest(): pl.pallas_call(lambda *refs: rest_kernel(whole, *refs), out_shape=(total,...  50.5 us
    ppermute x15, waiting for transfers between devices, to_cols(): return lax.ppermute(value, ('leaf',) + ROWS, pairs)  45.3 us
    ppermute x3, waiting for transfers between devices, along(): lax.ppermute(value, 'prow', [(r, (r + step) % prows) for r in range(prows)])  31.5 us
    pallas_call x4, Pallas kernels, spread_rows(): pl.pallas_call(rows_kernel, out_shape=jax.ShapeDtypeStruct((window, 2 * o...  15.5 us
    all_gather x4, starting transfers between devices, local(): lax.all_gather(rounded, 'prow', axis=0)  12 us
  transfers between devices with their start and end apart: 29, of which 8 were waited for; matrix products, arithmetic and copies ran while one was open for 5% of the time, Pallas kernels for 46%

profile of v1, /device:TPU:9, one launch (start us, length us, event | category | flops | bytes accessed | tf_op | source)
XLA Modules:
  0.0 519.6 jit_solution(17378115130729247946)
XLA Ops:
  10.1 37.1 %all-gather.13.cloned.1.call-done = f32[768,512]{1,0:T(8,128)} async-done(((f32[192,512]{1,0:T(8,128)}), f32[768,512]{1,0:T(8,128)}) %all-gather.13.cloned.1.call-update) | async-done | bytes 1572880 | tf_op jit(solution)/shard_map/all_gather | solution.py:493
  53.8 18.8 %collective-permute-done.1 = f32[192,256]{1,0:T(8,128)S(1)} collective-permute-done((f32[192,256]{1,0:T(8,128)S(1)}, f32[192,256]{1,0:T(8,128)S(1)}, u32[]{:S(2)}, u32[]{:S(2)}) %collective-permute-start.1) | collective-permute-done | bytes 196640 | tf_op jit(solution)/shard_map/ppermute | solution.py:483
  72.6 11.5 %collective-permute-done.2 = f32[192,256]{1,0:T(8,128)S(1)} collective-permute-done((f32[192,256]{1,0:T(8,128)S(1)}, f32[192,256]{1,0:T(8,128)S(1)}, u32[]{:S(2)}, u32[]{:S(2)}) %collective-permute-start.2) | collective-permute-done | bytes 196640 | tf_op jit(solution)/shard_map/ppermute | solution.py:483
  88.2 17.4 %all-gather.15.cloned.1.call-done = f32[768,768]{1,0:T(8,128)} async-done(((f32[192,768]{1,0:T(8,128)}), f32[768,768]{1,0:T(8,128)}) %all-gather.15.cloned.1.call-update) | async-done | bytes 2359312 | tf_op jit(solution)/shard_map/all_gather | solution.py:493
  105.5 2.4 slice.20
  108.8 16.5 %shard_map.76 = (f32[1536,256]{1,0:T(8,128)}, f32[768,256]{1,0:T(8,128)}, bf16[768,256]{1,0:T(8,128)(2,1)}, s32[1]{0:T(128)}) custom-call(s32[3]{0:T(128)} %pad_add_fusion.refs_0_, f32[4,192,256]{2,1,0:T(8,128)} %copy-done.13, f32[4,192,256]{2,1,0:T(8,128)} %copy-done.22, f32[768,1536]{1,0:T(8,128)} %bitcast.56, f32[4,192,512]{2,1,0:T(8,128)} %bitcast.61, ...), custom_call_target="tpu_custom_call" | custom-call | flops 12800000000 | bytes 5898240 | tf_op jit(solution)/shard_map/pallas_call | solution.py:245
  125.2 28.0 %shard_map.77 = (f32[1024,4096]{1,0:T(8,128)}, f32[768,3072]{1,0:T(8,128)}) custom-call(s32[2]{0:T(128)} %pad_add_fusion.1.refs_0_, f32[768,6144]{1,0:T(8,128)} %bitcast.53, f32[768,6144]{1,0:T(8,128)} %bitcast.54, s32[1,1,768]{2,1,0:T(1,128)} %get-tuple-element.50.refs_3_.own_links, s32[4,1,1,768]{3,2,1,0:T(1,128)} %get-tuple-element.52.refs_4_.own_links, ...), custom_call_target="tpu_custom_call" | custom-call | flops 22548578304 | bytes 42991616 | tf_op jit(solution)/shard_map/pallas_call | solution.py:327
  153.2 3.2 collective-permute-start.10
  156.5 11.9 %all-gather.19.cloned.1.call-start = ((), (), s32[]{:S(2)}) async-start(), calls=%async_computation.3 | async-start | bytes 3932160 | tf_op jit(solution)/shard_map/all_gather | solution.py:560
  168.4 34.0 %shard_map.78 = (f32[1536,512]{1,0:T(8,128)}, f32[768,512]{1,0:T(8,128)}, bf16[768,512]{1,0:T(8,128)(2,1)}, s32[1]{0:T(128)}) custom-call(s32[3]{0:T(128)} %pad_add_fusion.refs_0_, f32[4,192,512]{2,1,0:T(8,128)} %bitcast.62, f32[4,192,512]{2,1,0:T(8,128)} %collective-permute-done.4.refs_5_.refs_2_, f32[1536,256]{1,0:T(8,128)} %get-tuple-element.20.refs_6_.refs_3_, ...), custom_call_target="tpu_custom_call" | custom-call | flops 25600000000 | bytes 11796480 | tf_op jit(solution)/shard_map/pallas_call | solution.py:245
  204.0 26.3 %collective-permute-done.5.refs_2_ = f32[2,192,768]{2,1,0:T(8,128)S(1)} collective-permute-done((f32[2,192,768]{2,1,0:T(8,128)S(1)}, f32[2,192,768]{2,1,0:T(8,128)S(1)}, u32[]{:S(2)}, u32[]{:S(2)}) %collective-permute-start.5) | collective-permute-done | bytes 1179680 | tf_op jit(solution)/shard_map/ppermute | solution.py:462
  231.4 35.1 %shard_map.79 = (f32[768,512]{1,0:T(8,128)}, f32[768,512]{1,0:T(8,128)}, bf16[768,512]{1,0:T(8,128)(2,1)}, s32[1]{0:T(128)}) custom-call(s32[3]{0:T(128)} %pad_add_fusion.refs_0_, f32[2,192,768]{2,1,0:T(8,128)} %bitcast.45, f32[2,192,768]{2,1,0:T(8,128)} %copy-done.20, f32[1536,256]{1,0:T(8,128)} %get-tuple-element.20.refs_6_.refs_3_, ...), custom_call_target="tpu_custom_call" | custom-call | flops 25600000000 | bytes 7864320 | tf_op jit(solution)/shard_map/pallas_call | solution.py:245
  273.1 3.2 shard_map.80.rows
  278.4 4.6 shard_map.87.rows
  284.0 4.6 shard_map.86.rows
  288.6 2.7 constant_dynamic-slice_fusion.6
  293.1 3.4 constant_dynamic-slice_fusion.4
  297.2 22.5 %shard_map.81.total = f32[1024,4096]{1,0:T(8,128)} custom-call(s32[2]{0:T(128)} %pad_add_fusion.2.refs_0_, f32[768,3072]{1,0:T(8,128)} %collective-permute-done.10.refs_1_, s32[1,1,768]{2,1,0:T(1,128)} %get-tuple-element.49.other_links.refs_2_, s32[4,1,1,768]{3,2,1,0:T(1,128)} %get-tuple-element.51.refs_3_.other_links, ...), custom_call_target="tpu_custom_call", output_to_operand_aliasing={{}: (4, {})} | custom-call | flops 22548578304 | bytes 42991616 | tf_op jit(solution)/shard_map/pallas_call | solution.py:327
  320.9 14.1 %shard_map.82.total = f32[1024,4096]{1,0:T(8,128)} custom-call(s32[2]{0:T(128)} %fusion.places, bf16[1024,512]{1,0:T(8,128)(2,1)} %shard_map.80.rows, bf16[2,768,256]{2,1,0:T(8,128)(2,1)} %get-tuple-element.44.own, bf16[2,768,256]{2,1,0:T(8,128)(2,1)} %collective-permute-done.9.other, ...), custom_call_target="tpu_custom_call", output_to_operand_aliasing={{}: (6, {})} | custom-call | flops 3758096384 | bytes 16777216 | tf_op jit(solution)/shard_map/pallas_call | solution.py:408
  335.0 14.0 %shard_map.83.refs_10_.total = f32[1024,4096]{1,0:T(8,128)} custom-call(s32[2]{0:T(128)} %fusion.1.places, bf16[1024,512]{1,0:T(8,128)(2,1)} %shard_map.80.rows, bf16[2,768,256]{2,1,0:T(8,128)(2,1)} %collective-permute-done.7.own, bf16[2,768,256]{2,1,0:T(8,128)(2,1)} %collective-permute-done.8.other, ...), custom_call_target="tpu_custom_call", output_to_operand_aliasing={{}: (6, {})} | custom-call | flops 3758096384 | bytes 16777216 | tf_op jit(solution)/shard_map/pallas_call | solution.py:408
  349.0 19.9 %shard_map.84 = (f32[384,256]{1,0:T(8,128)}, f32[768,256]{1,0:T(8,128)}, bf16[768,256]{1,0:T(8,128)(2,1)}, s32[1]{0:T(128)}) custom-call(s32[3]{0:T(128)} %pad_add_fusion.refs_0_, f32[2,192,768]{2,1,0:T(8,128)} %bitcast.46, f32[2,192,768]{2,1,0:T(8,128)} %copy-done.20, f32[1536,256]{1,0:T(8,128)} %get-tuple-element.20.refs_6_.refs_3_, ...), custom_call_target="tpu_custom_call" | custom-call | flops 12800000000 | bytes 2949120 | tf_op jit(solution)/shard_map/pallas_call | solution.py:245
  370.3 3.8 constant_dynamic-slice_fusion
  374.2 3.3 collective-permute-start.18
  377.6 18.0 %collective-permute-done.20.refs_0_.own = bf16[2,768,512]{2,1,0:T(8,128)(2,1)} collective-permute-done((bf16[2,768,512]{2,1,0:T(8,128)(2,1)S(1)}, bf16[2,768,512]{2,1,0:T(8,128)(2,1)}, u32[]{:S(2)}, u32[]{:S(2)}) %collective-permute-start.20) | collective-permute-done | bytes 1572896 | tf_op jit(solution)/shard_map/ppermute | solution.py:462
  397.8 17.4 %shard_map.88.total = f32[1024,4096]{1,0:T(8,128)} custom-call(s32[2]{0:T(128)} %fusion.places, bf16[1024,1024]{1,0:T(8,128)(2,1)} %shard_map.87.rows, bf16[2,768,512]{2,1,0:T(8,128)(2,1)} %copy-done, bf16[2,768,512]{2,1,0:T(8,128)(2,1)} %copy-done.1, s32[4,1,1,768]{3,2,1,0:T(1,128)} %get-tuple-element.52.refs_4_.own_links, ...), custom_call_target="tpu_custom_call", output_to_operand_aliasing={{}: (6, {})} | custom-call | flops 7516192768 | bytes 16777216 | tf_op jit(solution)/shard_map/pallas_call | solution.py:408
  415.2 17.5 %shard_map.89.total = f32[1024,4096]{1,0:T(8,128)} custom-call(s32[2]{0:T(128)} %fusion.1.places, bf16[1024,1024]{1,0:T(8,128)(2,1)} %shard_map.87.rows, bf16[2,768,512]{2,1,0:T(8,128)(2,1)} %collective-permute-done.20.refs_0_.own, bf16[2,768,512]{2,1,0:T(8,128)(2,1)} %collective-permute-done.21.refs_2_.other, ...), custom_call_target="tpu_custom_call", output_to_operand_aliasing={{}: (6, {})} | custom-call | flops 7516192768 | bytes 16777216 | tf_op jit(solution)/shard_map/pallas_call | solution.py:408
  434.8 2.6 maximum_bitcast_fusion
  438.2 3.1 shard_map.85.rows
  443.2 17.3 %shard_map.90.total = f32[1024,4096]{1,0:T(8,128)} custom-call(s32[2]{0:T(128)} %fusion.places, bf16[1024,1024]{1,0:T(8,128)(2,1)} %shard_map.86.rows, bf16[2,768,512]{2,1,0:T(8,128)(2,1)} %get-tuple-element.38.own, bf16[2,768,512]{2,1,0:T(8,128)(2,1)} %collective-permute-done.18.other, ...), custom_call_target="tpu_custom_call", output_to_operand_aliasing={{}: (6, {})} | custom-call | flops 7516192768 | bytes 16777216 | tf_op jit(solution)/shard_map/pallas_call | solution.py:408
  464.1 17.5 %shard_map.91.total = f32[1024,4096]{1,0:T(8,128)} custom-call(s32[2]{0:T(128)} %fusion.1.places, bf16[1024,1024]{1,0:T(8,128)(2,1)} %shard_map.86.rows, bf16[2,768,512]{2,1,0:T(8,128)(2,1)} %copy-done.7, bf16[2,768,512]{2,1,0:T(8,128)(2,1)} %collective-permute-done.17.other, ...), custom_call_target="tpu_custom_call", output_to_operand_aliasing={{}: (6, {})} | custom-call | flops 7516192768 | bytes 16777216 | tf_op jit(solution)/shard_map/pallas_call | solution.py:408
  482.6 14.0 %shard_map.92.total = f32[1024,4096]{1,0:T(8,128)} custom-call(s32[2]{0:T(128)} %fusion.places, bf16[1024,512]{1,0:T(8,128)(2,1)} %shard_map.85.rows, bf16[2,768,256]{2,1,0:T(8,128)(2,1)} %copy-done.2, bf16[2,768,256]{2,1,0:T(8,128)(2,1)} %copy-done.16, s32[4,1,1,768]{3,2,1,0:T(1,128)} %get-tuple-element.52.refs_4_.own_links, ...), custom_call_target="tpu_custom_call", output_to_operand_aliasing={{}: (6, {})} | custom-call | flops 3758096384 | bytes 16777216 | tf_op jit(solution)/shard_map/pallas_call | solution.py:408
  498.5 14.0 %shard_map.93 = f32[1024,4096]{1,0:T(8,128)} custom-call(s32[2]{0:T(128)} %fusion.1.places, bf16[1024,512]{1,0:T(8,128)(2,1)} %shard_map.85.rows, bf16[2,768,256]{2,1,0:T(8,128)(2,1)} %copy-done.15, bf16[2,768,256]{2,1,0:T(8,128)(2,1)} %copy-done.14, s32[4,1,1,768]{3,2,1,0:T(1,128)} %get-tuple-element.52.refs_4_.own_links, ...), custom_call_target="tpu_custom_call", output_to_operand_aliasing={{}: (6, {})} | custom-call | flops 3758096384 | bytes 16777216 | tf_op jit(solution)/shard_map/pallas_call | solution.py:408
  (124 shorter events, 41.2 us)
Async XLA Ops:
  7.2 40.0 %all-gather.13.cloned.1.call-start = ((), (), s32[]{:S(2)}) async-start(), calls=%async_computation | async-start | bytes 1966080 | tf_op jit(solution)/shard_map/all_gather | solution.py:493
  9.1 96.4 %all-gather.15.cloned.1.call-start = ((), (), s32[]{:S(2)}) async-start(), calls=%async_computation.1 | async-start | bytes 2949120 | tf_op jit(solution)/shard_map/all_gather | solution.py:493
  10.0 278.5 %all-gather.17.cloned.1.call-start = ((), (), s32[]{:S(2)}) async-start(), calls=%async_computation.2 | async-start | bytes 1966080 | tf_op jit(solution)/shard_map/all_gather | solution.py:560
  47.2 60.7 %collective-permute-start.4 = (f32[4,192,512]{2,1,0:T(8,128)}, f32[4,192,512]{2,1,0:T(8,128)}, u32[]{:S(2)}, u32[]{:S(2)}) collective-permute-start(f32[4,192,512]{2,1,0:T(8,128)} %bitcast.60), channel_id=1, source_target_pairs={{0,1},{1,0},{2,3},{3,2},{4,5},{5,4},{6,7},{7,6},{8,9},{9,8},{10,11... | collective-permute-start | bytes 4718600 | tf_op jit(solution)/shard_map/ppermute | solution.py:462
  48.4 5.4 %collective-permute-start = (f32[192,256]{1,0:T(8,128)S(1)}, f32[192,256]{1,0:T(8,128)S(1)}, u32[]{:S(2)}, u32[]{:S(2)}) collective-permute-start(f32[192,256]{1,0:T(8,128)S(1)} %get-tuple-element.46), channel_id=1, source_target_pairs={{0,2},{2,4},{4,6},{6,0},{1,3},{3,5},{5,7},{7,1},{8,10},{10,12},{12... | collective-permute-start | bytes 589832 | tf_op jit(solution)/shard_map/ppermute | solution.py:483
  49.8 22.8 %collective-permute-start.1 = (f32[192,256]{1,0:T(8,128)S(1)}, f32[192,256]{1,0:T(8,128)S(1)}, u32[]{:S(2)}, u32[]{:S(2)}) collective-permute-start(f32[192,256]{1,0:T(8,128)S(1)} %get-tuple-element.46), channel_id=1, source_target_pairs={{0,4},{2,6},{4,0},{6,2},{1,5},{3,7},{5,1},{7,3},{8,12},{10,14},{12... | collective-permute-start | bytes 589832 | tf_op jit(solution)/shard_map/ppermute | solution.py:483
  51.9 32.2 %collective-permute-start.2 = (f32[192,256]{1,0:T(8,128)S(1)}, f32[192,256]{1,0:T(8,128)S(1)}, u32[]{:S(2)}, u32[]{:S(2)}) collective-permute-start(f32[192,256]{1,0:T(8,128)S(1)} %get-tuple-element.46), channel_id=1, source_target_pairs={{0,6},{2,0},{4,2},{6,4},{1,7},{3,1},{5,3},{7,5},{8,14},{10,8},{12,... | collective-permute-start | bytes 589832 | tf_op jit(solution)/shard_map/ppermute | solution.py:483
  84.2 23.7 %collective-permute-start.3 = (f32[4,192,256]{2,1,0:T(8,128)S(1)}, f32[4,192,256]{2,1,0:T(8,128)S(1)}, u32[]{:S(2)}, u32[]{:S(2)}) collective-permute-start(f32[4,192,256]{2,1,0:T(8,128)S(1)} %pad_maximum_fusion.refs_1_), channel_id=1, source_target_pairs={{0,1},{1,0},{2,3},{3,2},{4,5},{5,4},{6,7},{7,6},{8,9},{9,8},{10,11... | collective-permute-start | bytes 2359304 | tf_op jit(solution)/shard_map/ppermute | solution.py:462
  153.2 143.8 %collective-permute-start.10 = (f32[768,3072]{1,0:T(8,128)}, f32[768,3072]{1,0:T(8,128)}, u32[]{:S(2)}, u32[]{:S(2)}) collective-permute-start(f32[768,3072]{1,0:T(8,128)} %get-tuple-element.29), channel_id=1, source_target_pairs={{0,8},{8,0},{16,24},{24,16},{1,9},{9,1},{17,25},{25,17},{2,10},{10... | collective-permute-start | bytes 28311560 | tf_op jit(solution)/shard_map/ppermute | solution.py:453
  156.5 136.6 %all-gather.19.cloned.1.call-start = ((), (), s32[]{:S(2)}) async-start(), calls=%async_computation.3 | async-start | bytes 3932160 | tf_op jit(solution)/shard_map/all_gather | solution.py:560
  168.4 34.1 %copy-start.9 = (f32[384,768]{1,0:T(8,128)S(1)}, f32[384,768]{1,0:T(8,128)}, u32[]{:S(2)}) copy-start(f32[384,768]{1,0:T(8,128)} %slice.20) | copy-start | bytes 3538948
  168.4 35.0 %copy-start.17 = (bf16[768,256]{1,0:T(8,128)(2,1)S(1)}, bf16[768,256]{1,0:T(8,128)(2,1)}, u32[]{:S(2)}) copy-start(bf16[768,256]{1,0:T(8,128)(2,1)} %get-tuple-element.27.own) | copy-start | bytes 1179652
  202.5 167.8 %all-gather.23.cloned.1.call-start = ((), (), s32[]{:S(2)}) async-start(), calls=%async_computation.5 | async-start | bytes 3932160 | tf_op jit(solution)/shard_map/all_gather | solution.py:560
  202.5 27.8 %collective-permute-start.5 = (f32[2,192,768]{2,1,0:T(8,128)S(1)}, f32[2,192,768]{2,1,0:T(8,128)S(1)}, u32[]{:S(2)}, u32[]{:S(2)}) collective-permute-start(f32[2,192,768]{2,1,0:T(8,128)S(1)} %bitcast.47), channel_id=1, source_target_pairs={{0,1},{1,0},{2,3},{3,2},{4,5},{5,4},{6,7},{7,6},{8,9},{9,8},{10,11... | collective-permute-start | bytes 3538952 | tf_op jit(solution)/shard_map/ppermute | solution.py:462
  203.5 68.8 %collective-permute-start.6 = (bf16[768,256]{1,0:T(8,128)(2,1)S(1)}, bf16[768,256]{1,0:T(8,128)(2,1)S(1)}, u32[]{:S(2)}, u32[]{:S(2)}) collective-permute-start(bf16[768,256]{1,0:T(8,128)(2,1)S(1)} %copy-done.17), channel_id=1, source_target_pairs={{0,8},{8,0},{16,24},{24,16},{1,9},{9,1},{17,25},{25,17},{2,10},{10... | collective-permute-start | bytes 1179656 | tf_op jit(solution)/shard_map/ppermute | solution.py:453
  203.7 74.7 %collective-permute-start.19 = (bf16[768,512]{1,0:T(8,128)(2,1)}, bf16[768,512]{1,0:T(8,128)(2,1)}, u32[]{:S(2)}, u32[]{:S(2)}) collective-permute-start(bf16[768,512]{1,0:T(8,128)(2,1)} %get-tuple-element.30.own), channel_id=1, source_target_pairs={{0,8},{8,0},{16,24},{24,16},{1,9},{9,1},{17,25},{25,17},{2,10},{10... | collective-permute-start | bytes 2359304 | tf_op jit(solution)/shard_map/ppermute | solution.py:453
  266.5 16.6 %collective-permute-start.15 = (bf16[768,512]{1,0:T(8,128)(2,1)}, bf16[768,512]{1,0:T(8,128)(2,1)S(1)}, u32[]{:S(2)}, u32[]{:S(2)}) collective-permute-start(bf16[768,512]{1,0:T(8,128)(2,1)} %get-tuple-element.36.own), channel_id=1, source_target_pairs={{0,8},{8,0},{16,24},{24,16},{1,9},{9,1},{17,25},{25,17},{2,10},{10... | collective-permute-start | bytes 2359304 | tf_op jit(solution)/shard_map/ppermute | solution.py:453
  276.3 165.0 %all-gather.21.cloned.1.call-start = ((), (), s32[]{:S(2)}) async-start(), calls=%async_computation.4 | async-start | bytes 1966080 | tf_op jit(solution)/shard_map/all_gather | solution.py:560
  291.3 28.4 %collective-permute-start.9 = (bf16[2,768,256]{2,1,0:T(8,128)(2,1)}, bf16[2,768,256]{2,1,0:T(8,128)(2,1)}, u32[]{:S(2)}, u32[]{:S(2)}) collective-permute-start(bf16[2,768,256]{2,1,0:T(8,128)(2,1)} %get-tuple-element.43), channel_id=1, source_target_pairs={{0,8},{1,9},{2,10},{3,11},{4,12},{5,13},{6,14},{7,15},{8,0},{9,1},... | collective-permute-start | bytes 2359304 | tf_op jit(solution)/shard_map/ppermute | solution.py:462
  291.3 43.7 %collective-permute-start.8 = (bf16[2,768,256]{2,1,0:T(8,128)(2,1)}, bf16[2,768,256]{2,1,0:T(8,128)(2,1)}, u32[]{:S(2)}, u32[]{:S(2)}) collective-permute-start(bf16[2,768,256]{2,1,0:T(8,128)(2,1)} %get-tuple-element.43), channel_id=1, source_target_pairs={{0,9},{1,8},{2,11},{3,10},{4,13},{5,12},{6,15},{7,14},{8,1},{9,0},... | collective-permute-start | bytes 2359304 | tf_op jit(solution)/shard_map/ppermute | solution.py:462
  292.0 43.0 %collective-permute-start.7 = (bf16[2,768,256]{2,1,0:T(8,128)(2,1)}, bf16[2,768,256]{2,1,0:T(8,128)(2,1)}, u32[]{:S(2)}, u32[]{:S(2)}) collective-permute-start(bf16[2,768,256]{2,1,0:T(8,128)(2,1)} %get-tuple-element.44.own), channel_id=1, source_target_pairs={{0,1},{1,0},{2,3},{3,2},{4,5},{5,4},{6,7},{7,6},{8,9},{9,8},{10,11... | collective-permute-start | bytes 2359304 | tf_op jit(solution)/shard_map/ppermute | solution.py:462
  296.5 99.9 %collective-permute-start.21 = (bf16[2,768,512]{2,1,0:T(8,128)(2,1)}, bf16[2,768,512]{2,1,0:T(8,128)(2,1)}, u32[]{:S(2)}, u32[]{:S(2)}) collective-permute-start(bf16[2,768,512]{2,1,0:T(8,128)(2,1)} %get-tuple-element.39.refs_1_), channel_id=1, source_target_pairs={{0,9},{1,8},{2,11},{3,10},{4,13},{5,12},{6,15},{7,14},{8,1},{9,0},... | collective-permute-start | bytes 4718600 | tf_op jit(solution)/shard_map/ppermute | solution.py:462
  297.0 99.7 %collective-permute-start.22 = (bf16[2,768,512]{2,1,0:T(8,128)(2,1)}, bf16[2,768,512]{2,1,0:T(8,128)(2,1)S(1)}, u32[]{:S(2)}, u32[]{:S(2)}) collective-permute-start(bf16[2,768,512]{2,1,0:T(8,128)(2,1)} %get-tuple-element.39.refs_1_), channel_id=1, source_target_pairs={{0,8},{1,9},{2,10},{3,11},{4,12},{5,13},{6,14},{7,15},{8,0},{9,1},... | collective-permute-start | bytes 4718600 | tf_op jit(solution)/shard_map/ppermute | solution.py:462
  319.7 75.9 %collective-permute-start.20 = (bf16[2,768,512]{2,1,0:T(8,128)(2,1)S(1)}, bf16[2,768,512]{2,1,0:T(8,128)(2,1)}, u32[]{:S(2)}, u32[]{:S(2)}) collective-permute-start(bf16[2,768,512]{2,1,0:T(8,128)(2,1)S(1)} %get-tuple-element.40.refs_0_.own), channel_id=1, source_target_pairs={{0,1},{1,0},{2,3},{3,2},{4,5},{5,4},{6,7},{7,6},{8,9},{9,8},{10,11... | collective-permute-start | bytes 4718600 | tf_op jit(solution)/shard_map/ppermute | solution.py:462
  370.3 25.3 %copy-start.18 = (bf16[768,256]{1,0:T(8,128)(2,1)S(1)}, bf16[768,256]{1,0:T(8,128)(2,1)}, u32[]{:S(2)}) copy-start(bf16[768,256]{1,0:T(8,128)(2,1)} %get-tuple-element.34.own) | copy-start | bytes 1179652
  374.2 69.0 %collective-permute-start.18 = (bf16[2,768,512]{2,1,0:T(8,128)(2,1)}, bf16[2,768,512]{2,1,0:T(8,128)(2,1)}, u32[]{:S(2)}, u32[]{:S(2)}) collective-permute-start(bf16[2,768,512]{2,1,0:T(8,128)(2,1)} %get-tuple-element.37), channel_id=1, source_target_pairs={{0,8},{1,9},{2,10},{3,11},{4,12},{5,13},{6,14},{7,15},{8,0},{9,1},... | collective-permute-start | bytes 4718600 | tf_op jit(solution)/shard_map/ppermute | solution.py:462
  377.5 85.5 %collective-permute-start.17 = (bf16[2,768,512]{2,1,0:T(8,128)(2,1)}, bf16[2,768,512]{2,1,0:T(8,128)(2,1)}, u32[]{:S(2)}, u32[]{:S(2)}) collective-permute-start(bf16[2,768,512]{2,1,0:T(8,128)(2,1)} %get-tuple-element.37), channel_id=1, source_target_pairs={{0,9},{1,8},{2,11},{3,10},{4,13},{5,12},{6,15},{7,14},{8,1},{9,0},... | collective-permute-start | bytes 4718600 | tf_op jit(solution)/shard_map/ppermute | solution.py:462
  395.6 41.8 %collective-permute-start.11 = (bf16[768,256]{1,0:T(8,128)(2,1)S(1)}, bf16[768,256]{1,0:T(8,128)(2,1)S(1)}, u32[]{:S(2)}, u32[]{:S(2)}) collective-permute-start(bf16[768,256]{1,0:T(8,128)(2,1)S(1)} %copy-done.18), channel_id=1, source_target_pairs={{0,8},{8,0},{16,24},{24,16},{1,9},{9,1},{17,25},{25,17},{2,10},{10... | collective-permute-start | bytes 1179656 | tf_op jit(solution)/shard_map/ppermute | solution.py:453
  396.4 66.5 %collective-permute-start.16 = (bf16[2,768,512]{2,1,0:T(8,128)(2,1)}, bf16[2,768,512]{2,1,0:T(8,128)(2,1)S(1)}, u32[]{:S(2)}, u32[]{:S(2)}) collective-permute-start(bf16[2,768,512]{2,1,0:T(8,128)(2,1)} %get-tuple-element.38.own), channel_id=1, source_target_pairs={{0,1},{1,0},{2,3},{3,2},{4,5},{5,4},{6,7},{7,6},{8,9},{9,8},{10,11... | collective-permute-start | bytes 4718600 | tf_op jit(solution)/shard_map/ppermute | solution.py:462
  442.8 38.9 %collective-permute-start.14 = (bf16[2,768,256]{2,1,0:T(8,128)(2,1)S(1)}, bf16[2,768,256]{2,1,0:T(8,128)(2,1)S(1)}, u32[]{:S(2)}, u32[]{:S(2)}) collective-permute-start(bf16[2,768,256]{2,1,0:T(8,128)(2,1)S(1)} %get-tuple-element.41), channel_id=1, source_target_pairs={{0,8},{1,9},{2,10},{3,11},{4,12},{5,13},{6,14},{7,15},{8,0},{9,1},... | collective-permute-start | bytes 2359304 | tf_op jit(solution)/shard_map/ppermute | solution.py:462
  460.5 36.1 %collective-permute-start.13 = (bf16[2,768,256]{2,1,0:T(8,128)(2,1)S(1)}, bf16[2,768,256]{2,1,0:T(8,128)(2,1)S(1)}, u32[]{:S(2)}, u32[]{:S(2)}) collective-permute-start(bf16[2,768,256]{2,1,0:T(8,128)(2,1)S(1)} %get-tuple-element.41), channel_id=1, source_target_pairs={{0,9},{1,8},{2,11},{3,10},{4,13},{5,12},{6,15},{7,14},{8,1},{9,0},... | collective-permute-start | bytes 2359304 | tf_op jit(solution)/shard_map/ppermute | solution.py:462
  461.7 34.9 %collective-permute-start.12 = (bf16[2,768,256]{2,1,0:T(8,128)(2,1)S(1)}, bf16[2,768,256]{2,1,0:T(8,128)(2,1)S(1)}, u32[]{:S(2)}, u32[]{:S(2)}) collective-permute-start(bf16[2,768,256]{2,1,0:T(8,128)(2,1)S(1)} %get-tuple-element.42.own), channel_id=1, source_target_pairs={{0,1},{1,0},{2,3},{3,2},{4,5},{5,4},{6,7},{7,6},{8,9},{9,8},{10,11... | collective-permute-start | bytes 2359304 | tf_op jit(solution)/shard_map/ppermute | solution.py:462
  (22 other events, 164.2 us)
Sparse Core Ops, SparseCore 0:
  10.1 37.0 all-gather.12
  49.3 56.1 all-gather.14
  156.6 36.4 all-gather.16
  202.6 61.6 all-gather.18
  276.4 61.3 all-gather.22
  370.4 38.9 all-gather.20

commit v2 on v0

--- a/solution.py
+++ b/solution.py
@@ -537,9 +537,7 @@
                 (column_blocks[0][-1], column_blocks[1][0]),
                 True,
             )
-            waits = (start_total, column_blocks[2][0])
-        elif p == 2:
-            waits = parts[0][1]
+            waits = (start_total,) + tuple(column_blocks[2])
         elif p == 3:
             total = add_rest(
                 start_total,

time: 509 us -> 503 us (0.988)
  starting transfers between devices: 53.5 us -> 35.3 us
  waiting for transfers between devices: 94.2 us -> 105 us
    all_gather x2, waiting for transfers between devices: 12.9 us -> 53.3 us  [local(): mine = lax.all_gather(mine, 'prow', axis=0)[s // across_z:]]
    ppermute x15, waiting for transfers between devices: 52 us -> 17.5 us  [to_cols(): return lax.ppermute(value, ('leaf',) + ROWS, pairs)]
    ppermute x5, starting transfers between devices: 24.2 us -> 6.35 us  [to_sibling(): return lax.ppermute(value, 'leaf', [(g, g ^ 1) for g in range(leaves)])]
    unnamed x46 -> x52, local copies, waits for them, and re-layouts: 8.84 us -> 11.5 us
  transfers between devices with their start and end apart: 29 -> 29, of which waited for: 11 -> 8; matrix products, arithmetic and copies ran while one was open for 5% -> 5% of each run, Pallas kernels for 57% -> 57%
where the time goes in v2:
time: 503 us; the launch traced here: 497 us
  Pallas kernels  297 us (59%)
  waiting for transfers between devices  105 us (21%)
  starting transfers between devices  35.3 us (7%)
  local copies, waits for them, and re-layouts  31.4 us (6%)
  between operations  18.4 us (4%)
  other arithmetic  8.96 us (2%)
    pallas_call x8, Pallas kernels, update_windows(): pl.pallas_call(update_kernel, out_shape=jax.ShapeDtypeStruct(total.shape,...  126 us
    pallas_call x4, Pallas kernels, factor_panel(): pl.pallas_call(lambda *refs: panel_kernel(first, base, bases, len(shares)...  106 us
    all_gather x2, waiting for transfers between devices, local(): mine = lax.all_gather(mine, 'prow', axis=0)[s // across_z:]  53.3 us
    pallas_call x2, Pallas kernels, add_rest(): pl.pallas_call(lambda *refs: rest_kernel(whole, *refs), out_shape=(total,...  50.7 us
    ppermute x3, waiting for transfers between devices, along(): lax.ppermute(value, 'prow', [(r, (r + step) % prows) for r in range(prows)])  34.1 us
    ppermute x15, waiting for transfers between devices, to_cols(): return lax.ppermute(value, ('leaf',) + ROWS, pairs)  17.5 us
    pallas_call x4, Pallas kernels, spread_rows(): pl.pallas_call(rows_kernel, out_shape=jax.ShapeDtypeStruct((window, 2 * o...  15.3 us
    ppermute x15, starting transfers between devices, to_cols(): return lax.ppermute(value, ('leaf',) + ROWS, pairs)  13 us
  transfers between devices with their start and end apart: 29, of which 8 were waited for; matrix products, arithmetic and copies ran while one was open for 5% of the time, Pallas kernels for 57%

profile of v2, /device:TPU:9, one launch (start us, length us, event | category | flops | bytes accessed | tf_op | source)
XLA Modules:
  0.0 496.5 jit_solution(7244767319743741242)
XLA Ops:
  7.2 1.9 slice.18
  14.0 2.0 collective-permute-done
  15.9 19.5 %collective-permute-done.1 = f32[192,256]{1,0:T(8,128)S(1)} collective-permute-done((f32[192,256]{1,0:T(8,128)S(1)}, f32[192,256]{1,0:T(8,128)S(1)}, u32[]{:S(2)}, u32[]{:S(2)}) %collective-permute-start.1) | collective-permute-done | bytes 196640 | tf_op jit(solution)/shard_map/ppermute | solution.py:483
  35.5 12.6 %collective-permute-done.2 = f32[192,256]{1,0:T(8,128)S(1)} collective-permute-done((f32[192,256]{1,0:T(8,128)S(1)}, f32[192,256]{1,0:T(8,128)S(1)}, u32[]{:S(2)}, u32[]{:S(2)}) %collective-permute-start.2) | collective-permute-done | bytes 196640 | tf_op jit(solution)/shard_map/ppermute | solution.py:483
  52.4 2.5 all-gather.13.cloned.1.call-done
  56.4 50.8 %all-gather.15.cloned.1.call-done = f32[768,768]{1,0:T(8,128)} async-done(((f32[192,768]{1,0:T(8,128)}), f32[768,768]{1,0:T(8,128)}) %all-gather.15.cloned.1.call-update) | async-done | bytes 2359312 | tf_op jit(solution)/shard_map/all_gather | solution.py:493
  110.7 28.0 %shard_map.76 = (f32[1024,4096]{1,0:T(8,128)}, f32[768,3072]{1,0:T(8,128)}) custom-call(s32[2]{0:T(128)} %pad_add_fusion.1.refs_0_, f32[768,6144]{1,0:T(8,128)} %bitcast.55, f32[768,6144]{1,0:T(8,128)} %bitcast.56, s32[1,1,768]{2,1,0:T(1,128)} %get-tuple-element.50.refs_3_.own_links, s32[4,1,1,768]{3,2,1,0:T(1,128)} %get-tuple-element.52.refs_4_.own_links, ...), custom_call_target="tpu_custom_call" | custom-call | flops 22548578304 | bytes 42991616 | tf_op jit(solution)/shard_map/pallas_call | solution.py:327
  138.7 4.1 collective-permute-start.10
  144.5 16.5 %shard_map.77 = (f32[1536,256]{1,0:T(8,128)}, f32[768,256]{1,0:T(8,128)}, bf16[768,256]{1,0:T(8,128)(2,1)}, s32[1]{0:T(128)}) custom-call(s32[3]{0:T(128)} %pad_add_fusion.refs_0_, f32[4,192,256]{2,1,0:T(8,128)} %copy-done.13, f32[4,192,256]{2,1,0:T(8,128)} %copy-done.23, f32[768,1536]{1,0:T(8,128)} %bitcast.58, ...), custom_call_target="tpu_custom_call" | custom-call | flops 12800000000 | bytes 5898240 | tf_op jit(solution)/shard_map/pallas_call | solution.py:245
  160.9 11.9 %all-gather.19.cloned.1.call-start = ((), (), s32[]{:S(2)}) async-start(), calls=%async_computation.3 | async-start | bytes 3932160 | tf_op jit(solution)/shard_map/all_gather | solution.py:558
  173.9 33.9 %shard_map.78 = (f32[1536,512]{1,0:T(8,128)}, f32[768,512]{1,0:T(8,128)}, bf16[768,512]{1,0:T(8,128)(2,1)}, s32[1]{0:T(128)}) custom-call(s32[3]{0:T(128)} %pad_add_fusion.refs_0_, f32[4,192,512]{2,1,0:T(8,128)} %bitcast.64, f32[4,192,512]{2,1,0:T(8,128)} %copy-done.20, f32[1536,256]{1,0:T(8,128)} %get-tuple-element.21.refs_3_, ...), custom_call_target="tpu_custom_call" | custom-call | flops 25600000000 | bytes 11796480 | tf_op jit(solution)/shard_map/pallas_call | solution.py:245
  208.6 35.3 %shard_map.79 = (f32[768,512]{1,0:T(8,128)}, f32[768,512]{1,0:T(8,128)}, bf16[768,512]{1,0:T(8,128)(2,1)}, s32[1]{0:T(128)}) custom-call(s32[3]{0:T(128)} %pad_add_fusion.refs_0_, f32[2,192,768]{2,1,0:T(8,128)} %bitcast.47, f32[2,192,768]{2,1,0:T(8,128)} %copy-done.21, f32[1536,256]{1,0:T(8,128)} %get-tuple-element.21.refs_3_, ...), custom_call_target="tpu_custom_call" | custom-call | flops 25600000000 | bytes 7864320 | tf_op jit(solution)/shard_map/pallas_call | solution.py:245
  252.3 3.1 shard_map.80.rows
  256.3 4.6 shard_map.87.rows
  260.9 4.5 shard_map.86.rows
  265.4 2.7 constant_dynamic-slice_fusion.6
  270.0 3.4 constant_dynamic-slice_fusion.4
  274.2 22.7 %shard_map.81.total = f32[1024,4096]{1,0:T(8,128)} custom-call(s32[2]{0:T(128)} %pad_add_fusion.2.refs_0_, f32[768,3072]{1,0:T(8,128)} %collective-permute-done.10.refs_1_, s32[1,1,768]{2,1,0:T(1,128)} %get-tuple-element.49.other_links.refs_2_, s32[4,1,1,768]{3,2,1,0:T(1,128)} %get-tuple-element.51.refs_3_.other_links, ...), custom_call_target="tpu_custom_call", output_to_operand_aliasing={{}: (4, {})} | custom-call | flops 22548578304 | bytes 42991616 | tf_op jit(solution)/shard_map/pallas_call | solution.py:327
  298.3 14.1 %shard_map.82.total = f32[1024,4096]{1,0:T(8,128)} custom-call(s32[2]{0:T(128)} %fusion.places, bf16[1024,512]{1,0:T(8,128)(2,1)} %shard_map.80.rows, bf16[2,768,256]{2,1,0:T(8,128)(2,1)} %get-tuple-element.44.own, bf16[2,768,256]{2,1,0:T(8,128)(2,1)} %collective-permute-done.9.other, ...), custom_call_target="tpu_custom_call", output_to_operand_aliasing={{}: (6, {})} | custom-call | flops 3758096384 | bytes 16777216 | tf_op jit(solution)/shard_map/pallas_call | solution.py:408
  312.4 14.0 %shard_map.83.refs_10_.total = f32[1024,4096]{1,0:T(8,128)} custom-call(s32[2]{0:T(128)} %fusion.1.places, bf16[1024,512]{1,0:T(8,128)(2,1)} %shard_map.80.rows, bf16[2,768,256]{2,1,0:T(8,128)(2,1)} %collective-permute-done.7.own, bf16[2,768,256]{2,1,0:T(8,128)(2,1)} %collective-permute-done.8.other, ...), custom_call_target="tpu_custom_call", output_to_operand_aliasing={{}: (6, {})} | custom-call | flops 3758096384 | bytes 16777216 | tf_op jit(solution)/shard_map/pallas_call | solution.py:408
  326.4 19.9 %shard_map.84 = (f32[384,256]{1,0:T(8,128)}, f32[768,256]{1,0:T(8,128)}, bf16[768,256]{1,0:T(8,128)(2,1)}, s32[1]{0:T(128)}) custom-call(s32[3]{0:T(128)} %pad_add_fusion.refs_0_, f32[2,192,768]{2,1,0:T(8,128)} %bitcast.49, f32[2,192,768]{2,1,0:T(8,128)} %copy-done.21, f32[1536,256]{1,0:T(8,128)} %get-tuple-element.21.refs_3_, ...), custom_call_target="tpu_custom_call" | custom-call | flops 12800000000 | bytes 2949120 | tf_op jit(solution)/shard_map/pallas_call | solution.py:245
  347.8 3.8 constant_dynamic-slice_fusion
  351.6 3.7 collective-permute-start.18
  355.4 16.7 %collective-permute-done.20.refs_0_.own = bf16[2,768,512]{2,1,0:T(8,128)(2,1)} collective-permute-done((bf16[2,768,512]{2,1,0:T(8,128)(2,1)S(1)}, bf16[2,768,512]{2,1,0:T(8,128)(2,1)}, u32[]{:S(2)}, u32[]{:S(2)}) %collective-permute-start.20) | collective-permute-done | bytes 1572896 | tf_op jit(solution)/shard_map/ppermute | solution.py:462
  374.9 17.3 %shard_map.88.total = f32[1024,4096]{1,0:T(8,128)} custom-call(s32[2]{0:T(128)} %fusion.places, bf16[1024,1024]{1,0:T(8,128)(2,1)} %shard_map.87.rows, bf16[2,768,512]{2,1,0:T(8,128)(2,1)} %copy-done, bf16[2,768,512]{2,1,0:T(8,128)(2,1)} %copy-done.1, s32[4,1,1,768]{3,2,1,0:T(1,128)} %get-tuple-element.52.refs_4_.own_links, ...), custom_call_target="tpu_custom_call", output_to_operand_aliasing={{}: (6, {})} | custom-call | flops 7516192768 | bytes 16777216 | tf_op jit(solution)/shard_map/pallas_call | solution.py:408
  392.2 17.5 %shard_map.89.total = f32[1024,4096]{1,0:T(8,128)} custom-call(s32[2]{0:T(128)} %fusion.1.places, bf16[1024,1024]{1,0:T(8,128)(2,1)} %shard_map.87.rows, bf16[2,768,512]{2,1,0:T(8,128)(2,1)} %collective-permute-done.20.refs_0_.own, bf16[2,768,512]{2,1,0:T(8,128)(2,1)} %collective-permute-done.21.refs_2_.other, ...), custom_call_target="tpu_custom_call", output_to_operand_aliasing={{}: (6, {})} | custom-call | flops 7516192768 | bytes 16777216 | tf_op jit(solution)/shard_map/pallas_call | solution.py:408
  411.8 2.6 maximum_bitcast_fusion
  415.2 3.1 shard_map.85.rows
  420.2 17.3 %shard_map.90.total = f32[1024,4096]{1,0:T(8,128)} custom-call(s32[2]{0:T(128)} %fusion.places, bf16[1024,1024]{1,0:T(8,128)(2,1)} %shard_map.86.rows, bf16[2,768,512]{2,1,0:T(8,128)(2,1)} %get-tuple-element.38.own, bf16[2,768,512]{2,1,0:T(8,128)(2,1)} %collective-permute-done.18.other, ...), custom_call_target="tpu_custom_call", output_to_operand_aliasing={{}: (6, {})} | custom-call | flops 7516192768 | bytes 16777216 | tf_op jit(solution)/shard_map/pallas_call | solution.py:408
  440.5 17.5 %shard_map.91.total = f32[1024,4096]{1,0:T(8,128)} custom-call(s32[2]{0:T(128)} %fusion.1.places, bf16[1024,1024]{1,0:T(8,128)(2,1)} %shard_map.86.rows, bf16[2,768,512]{2,1,0:T(8,128)(2,1)} %copy-done.7, bf16[2,768,512]{2,1,0:T(8,128)(2,1)} %collective-permute-done.17.other, ...), custom_call_target="tpu_custom_call", output_to_operand_aliasing={{}: (6, {})} | custom-call | flops 7516192768 | bytes 16777216 | tf_op jit(solution)/shard_map/pallas_call | solution.py:408
  458.9 14.0 %shard_map.92.total = f32[1024,4096]{1,0:T(8,128)} custom-call(s32[2]{0:T(128)} %fusion.places, bf16[1024,512]{1,0:T(8,128)(2,1)} %shard_map.85.rows, bf16[2,768,256]{2,1,0:T(8,128)(2,1)} %copy-done.2, bf16[2,768,256]{2,1,0:T(8,128)(2,1)} %copy-done.16, s32[4,1,1,768]{3,2,1,0:T(1,128)} %get-tuple-element.52.refs_4_.own_links, ...), custom_call_target="tpu_custom_call", output_to_operand_aliasing={{}: (6, {})} | custom-call | flops 3758096384 | bytes 16777216 | tf_op jit(solution)/shard_map/pallas_call | solution.py:408
  475.4 14.0 %shard_map.93 = f32[1024,4096]{1,0:T(8,128)} custom-call(s32[2]{0:T(128)} %fusion.1.places, bf16[1024,512]{1,0:T(8,128)(2,1)} %shard_map.85.rows, bf16[2,768,256]{2,1,0:T(8,128)(2,1)} %copy-done.15, bf16[2,768,256]{2,1,0:T(8,128)(2,1)} %copy-done.14, s32[4,1,1,768]{3,2,1,0:T(1,128)} %get-tuple-element.52.refs_4_.own_links, ...), custom_call_target="tpu_custom_call", output_to_operand_aliasing={{}: (6, {})} | custom-call | flops 3758096384 | bytes 16777216 | tf_op jit(solution)/shard_map/pallas_call | solution.py:408
  (126 shorter events, 42.6 us)
Async XLA Ops:
  7.2 47.7 %all-gather.13.cloned.1.call-start = ((), (), s32[]{:S(2)}) async-start(), calls=%async_computation | async-start | bytes 1966080 | tf_op jit(solution)/shard_map/all_gather | solution.py:493
  9.1 98.1 %all-gather.15.cloned.1.call-start = ((), (), s32[]{:S(2)}) async-start(), calls=%async_computation.1 | async-start | bytes 2949120 | tf_op jit(solution)/shard_map/all_gather | solution.py:493
  10.0 255.4 %all-gather.17.cloned.1.call-start = ((), (), s32[]{:S(2)}) async-start(), calls=%async_computation.2 | async-start | bytes 1966080 | tf_op jit(solution)/shard_map/all_gather | solution.py:558
  10.1 5.8 %collective-permute-start = (f32[192,256]{1,0:T(8,128)S(1)}, f32[192,256]{1,0:T(8,128)S(1)}, u32[]{:S(2)}, u32[]{:S(2)}) collective-permute-start(f32[192,256]{1,0:T(8,128)S(1)} %get-tuple-element.46), channel_id=1, source_target_pairs={{0,2},{2,4},{4,6},{6,0},{1,3},{3,5},{5,7},{7,1},{8,10},{10,12},{12... | collective-permute-start | bytes 589832 | tf_op jit(solution)/shard_map/ppermute | solution.py:483
  11.5 24.0 %collective-permute-start.1 = (f32[192,256]{1,0:T(8,128)S(1)}, f32[192,256]{1,0:T(8,128)S(1)}, u32[]{:S(2)}, u32[]{:S(2)}) collective-permute-start(f32[192,256]{1,0:T(8,128)S(1)} %get-tuple-element.46), channel_id=1, source_target_pairs={{0,4},{2,6},{4,0},{6,2},{1,5},{3,7},{5,1},{7,3},{8,12},{10,14},{12... | collective-permute-start | bytes 589832 | tf_op jit(solution)/shard_map/ppermute | solution.py:483
  12.6 35.5 %collective-permute-start.2 = (f32[192,256]{1,0:T(8,128)S(1)}, f32[192,256]{1,0:T(8,128)S(1)}, u32[]{:S(2)}, u32[]{:S(2)}) collective-permute-start(f32[192,256]{1,0:T(8,128)S(1)} %get-tuple-element.46), channel_id=1, source_target_pairs={{0,6},{2,0},{4,2},{6,4},{1,7},{3,1},{5,3},{7,5},{8,14},{10,8},{12,... | collective-permute-start | bytes 589832 | tf_op jit(solution)/shard_map/ppermute | solution.py:483
  48.1 90.6 %copy-start.13 = (f32[4,192,256]{2,1,0:T(8,128)}, f32[4,192,256]{2,1,0:T(8,128)S(1)}, u32[]{:S(2)}) copy-start(f32[4,192,256]{2,1,0:T(8,128)S(1)} %pad_maximum_fusion.refs_1_) | copy-start | bytes 2359300
  48.1 61.7 %collective-permute-start.3 = (f32[4,192,256]{2,1,0:T(8,128)S(1)}, f32[4,192,256]{2,1,0:T(8,128)S(1)}, u32[]{:S(2)}, u32[]{:S(2)}) collective-permute-start(f32[4,192,256]{2,1,0:T(8,128)S(1)} %pad_maximum_fusion.refs_1_), channel_id=1, source_target_pairs={{0,1},{1,0},{2,3},{3,2},{4,5},{5,4},{6,7},{7,6},{8,9},{9,8},{10,11... | collective-permute-start | bytes 2359304 | tf_op jit(solution)/shard_map/ppermute | solution.py:462
  54.9 118.0 %collective-permute-start.5 = (f32[4,192,512]{2,1,0:T(8,128)}, f32[4,192,512]{2,1,0:T(8,128)S(1)}, u32[]{:S(2)}, u32[]{:S(2)}) collective-permute-start(f32[4,192,512]{2,1,0:T(8,128)} %bitcast.62), channel_id=1, source_target_pairs={{0,1},{1,0},{2,3},{3,2},{4,5},{5,4},{6,7},{7,6},{8,9},{9,8},{10,11... | collective-permute-start | bytes 4718600 | tf_op jit(solution)/shard_map/ppermute | solution.py:462
  108.5 30.2 %copy-start.9 = (f32[384,768]{1,0:T(8,128)}, f32[384,768]{1,0:T(8,128)S(1)}, u32[]{:S(2)}) copy-start(f32[384,768]{1,0:T(8,128)S(1)} %slice.20) | copy-start | bytes 3538948
  108.6 34.9 %collective-permute-start.4 = (f32[2,192,768]{2,1,0:T(8,128)S(1)}, f32[2,192,768]{2,1,0:T(8,128)S(1)}, u32[]{:S(2)}, u32[]{:S(2)}) collective-permute-start(f32[2,192,768]{2,1,0:T(8,128)S(1)} %bitcast.44), channel_id=1, source_target_pairs={{0,1},{1,0},{2,3},{3,2},{4,5},{5,4},{6,7},{7,6},{8,9},{9,8},{10,11... | collective-permute-start | bytes 3538952 | tf_op jit(solution)/shard_map/ppermute | solution.py:462
  138.7 135.4 %collective-permute-start.10 = (f32[768,3072]{1,0:T(8,128)}, f32[768,3072]{1,0:T(8,128)}, u32[]{:S(2)}, u32[]{:S(2)}) collective-permute-start(f32[768,3072]{1,0:T(8,128)} %get-tuple-element.29), channel_id=1, source_target_pairs={{0,8},{8,0},{16,24},{24,16},{1,9},{9,1},{17,25},{25,17},{2,10},{10... | collective-permute-start | bytes 28311560 | tf_op jit(solution)/shard_map/ppermute | solution.py:453
  160.9 109.0 %all-gather.19.cloned.1.call-start = ((), (), s32[]{:S(2)}) async-start(), calls=%async_computation.3 | async-start | bytes 3932160 | tf_op jit(solution)/shard_map/all_gather | solution.py:558
  207.9 139.9 %all-gather.23.cloned.1.call-start = ((), (), s32[]{:S(2)}) async-start(), calls=%async_computation.5 | async-start | bytes 3932160 | tf_op jit(solution)/shard_map/all_gather | solution.py:558
  208.5 46.9 %collective-permute-start.19 = (bf16[768,512]{1,0:T(8,128)(2,1)}, bf16[768,512]{1,0:T(8,128)(2,1)S(1)}, u32[]{:S(2)}, u32[]{:S(2)}) collective-permute-start(bf16[768,512]{1,0:T(8,128)(2,1)} %get-tuple-element.30.own), channel_id=1, source_target_pairs={{0,8},{8,0},{16,24},{24,16},{1,9},{9,1},{17,25},{25,17},{2,10},{10... | collective-permute-start | bytes 2359304 | tf_op jit(solution)/shard_map/ppermute | solution.py:453
  208.5 36.5 %copy-start.17 = (bf16[768,256]{1,0:T(8,128)(2,1)S(1)}, bf16[768,256]{1,0:T(8,128)(2,1)}, u32[]{:S(2)}) copy-start(bf16[768,256]{1,0:T(8,128)(2,1)} %get-tuple-element.27.own) | copy-start | bytes 1179652
  243.9 17.1 %collective-permute-start.15 = (bf16[768,512]{1,0:T(8,128)(2,1)}, bf16[768,512]{1,0:T(8,128)(2,1)}, u32[]{:S(2)}, u32[]{:S(2)}) collective-permute-start(bf16[768,512]{1,0:T(8,128)(2,1)} %get-tuple-element.36.own), channel_id=1, source_target_pairs={{0,8},{8,0},{16,24},{24,16},{1,9},{9,1},{17,25},{25,17},{2,10},{10... | collective-permute-start | bytes 2359304 | tf_op jit(solution)/shard_map/ppermute | solution.py:453
  245.0 6.6 %collective-permute-start.6 = (bf16[768,256]{1,0:T(8,128)(2,1)S(1)}, bf16[768,256]{1,0:T(8,128)(2,1)S(1)}, u32[]{:S(2)}, u32[]{:S(2)}) collective-permute-start(bf16[768,256]{1,0:T(8,128)(2,1)S(1)} %copy-done.17), channel_id=1, source_target_pairs={{0,8},{8,0},{16,24},{24,16},{1,9},{9,1},{17,25},{25,17},{2,10},{10... | collective-permute-start | bytes 1179656 | tf_op jit(solution)/shard_map/ppermute | solution.py:453
  248.0 170.3 %all-gather.21.cloned.1.call-start = ((), (), s32[]{:S(2)}) async-start(), calls=%async_computation.4 | async-start | bytes 1966080 | tf_op jit(solution)/shard_map/all_gather | solution.py:558
  268.1 28.8 %collective-permute-start.9 = (bf16[2,768,256]{2,1,0:T(8,128)(2,1)}, bf16[2,768,256]{2,1,0:T(8,128)(2,1)}, u32[]{:S(2)}, u32[]{:S(2)}) collective-permute-start(bf16[2,768,256]{2,1,0:T(8,128)(2,1)} %get-tuple-element.43), channel_id=1, source_target_pairs={{0,8},{1,9},{2,10},{3,11},{4,12},{5,13},{6,14},{7,15},{8,0},{9,1},... | collective-permute-start | bytes 2359304 | tf_op jit(solution)/shard_map/ppermute | solution.py:462
  268.6 43.8 %collective-permute-start.8 = (bf16[2,768,256]{2,1,0:T(8,128)(2,1)}, bf16[2,768,256]{2,1,0:T(8,128)(2,1)}, u32[]{:S(2)}, u32[]{:S(2)}) collective-permute-start(bf16[2,768,256]{2,1,0:T(8,128)(2,1)} %get-tuple-element.43), channel_id=1, source_target_pairs={{0,9},{1,8},{2,11},{3,10},{4,13},{5,12},{6,15},{7,14},{8,1},{9,0},... | collective-permute-start | bytes 2359304 | tf_op jit(solution)/shard_map/ppermute | solution.py:462
  268.6 43.7 %collective-permute-start.7 = (bf16[2,768,256]{2,1,0:T(8,128)(2,1)}, bf16[2,768,256]{2,1,0:T(8,128)(2,1)}, u32[]{:S(2)}, u32[]{:S(2)}) collective-permute-start(bf16[2,768,256]{2,1,0:T(8,128)(2,1)} %get-tuple-element.44.own), channel_id=1, source_target_pairs={{0,1},{1,0},{2,3},{3,2},{4,5},{5,4},{6,7},{7,6},{8,9},{9,8},{10,11... | collective-permute-start | bytes 2359304 | tf_op jit(solution)/shard_map/ppermute | solution.py:462
  273.3 100.3 %collective-permute-start.21 = (bf16[2,768,512]{2,1,0:T(8,128)(2,1)}, bf16[2,768,512]{2,1,0:T(8,128)(2,1)}, u32[]{:S(2)}, u32[]{:S(2)}) collective-permute-start(bf16[2,768,512]{2,1,0:T(8,128)(2,1)} %get-tuple-element.39.refs_1_), channel_id=1, source_target_pairs={{0,9},{1,8},{2,11},{3,10},{4,13},{5,12},{6,15},{7,14},{8,1},{9,0},... | collective-permute-start | bytes 4718600 | tf_op jit(solution)/shard_map/ppermute | solution.py:462
  274.1 99.7 %collective-permute-start.22 = (bf16[2,768,512]{2,1,0:T(8,128)(2,1)}, bf16[2,768,512]{2,1,0:T(8,128)(2,1)S(1)}, u32[]{:S(2)}, u32[]{:S(2)}) collective-permute-start(bf16[2,768,512]{2,1,0:T(8,128)(2,1)} %get-tuple-element.39.refs_1_), channel_id=1, source_target_pairs={{0,8},{1,9},{2,10},{3,11},{4,12},{5,13},{6,14},{7,15},{8,0},{9,1},... | collective-permute-start | bytes 4718600 | tf_op jit(solution)/shard_map/ppermute | solution.py:462
  296.9 75.1 %collective-permute-start.20 = (bf16[2,768,512]{2,1,0:T(8,128)(2,1)S(1)}, bf16[2,768,512]{2,1,0:T(8,128)(2,1)}, u32[]{:S(2)}, u32[]{:S(2)}) collective-permute-start(bf16[2,768,512]{2,1,0:T(8,128)(2,1)S(1)} %get-tuple-element.40.refs_0_.own), channel_id=1, source_target_pairs={{0,1},{1,0},{2,3},{3,2},{4,5},{5,4},{6,7},{7,6},{8,9},{9,8},{10,11... | collective-permute-start | bytes 4718600 | tf_op jit(solution)/shard_map/ppermute | solution.py:462
  351.6 68.6 %collective-permute-start.18 = (bf16[2,768,512]{2,1,0:T(8,128)(2,1)}, bf16[2,768,512]{2,1,0:T(8,128)(2,1)}, u32[]{:S(2)}, u32[]{:S(2)}) collective-permute-start(bf16[2,768,512]{2,1,0:T(8,128)(2,1)} %get-tuple-element.37), channel_id=1, source_target_pairs={{0,8},{1,9},{2,10},{3,11},{4,12},{5,13},{6,14},{7,15},{8,0},{9,1},... | collective-permute-start | bytes 4718600 | tf_op jit(solution)/shard_map/ppermute | solution.py:462
  355.3 84.0 %collective-permute-start.17 = (bf16[2,768,512]{2,1,0:T(8,128)(2,1)}, bf16[2,768,512]{2,1,0:T(8,128)(2,1)}, u32[]{:S(2)}, u32[]{:S(2)}) collective-permute-start(bf16[2,768,512]{2,1,0:T(8,128)(2,1)} %get-tuple-element.37), channel_id=1, source_target_pairs={{0,9},{1,8},{2,11},{3,10},{4,13},{5,12},{6,15},{7,14},{8,1},{9,0},... | collective-permute-start | bytes 4718600 | tf_op jit(solution)/shard_map/ppermute | solution.py:462
  372.0 42.4 %collective-permute-start.11 = (bf16[768,256]{1,0:T(8,128)(2,1)S(1)}, bf16[768,256]{1,0:T(8,128)(2,1)S(1)}, u32[]{:S(2)}, u32[]{:S(2)}) collective-permute-start(bf16[768,256]{1,0:T(8,128)(2,1)S(1)} %copy-done.18), channel_id=1, source_target_pairs={{0,8},{8,0},{16,24},{24,16},{1,9},{9,1},{17,25},{25,17},{2,10},{10... | collective-permute-start | bytes 1179656 | tf_op jit(solution)/shard_map/ppermute | solution.py:453
  373.6 65.7 %collective-permute-start.16 = (bf16[2,768,512]{2,1,0:T(8,128)(2,1)}, bf16[2,768,512]{2,1,0:T(8,128)(2,1)S(1)}, u32[]{:S(2)}, u32[]{:S(2)}) collective-permute-start(bf16[2,768,512]{2,1,0:T(8,128)(2,1)} %get-tuple-element.38.own), channel_id=1, source_target_pairs={{0,1},{1,0},{2,3},{3,2},{4,5},{5,4},{6,7},{7,6},{8,9},{9,8},{10,11... | collective-permute-start | bytes 4718600 | tf_op jit(solution)/shard_map/ppermute | solution.py:462
  419.8 38.2 %collective-permute-start.14 = (bf16[2,768,256]{2,1,0:T(8,128)(2,1)S(1)}, bf16[2,768,256]{2,1,0:T(8,128)(2,1)S(1)}, u32[]{:S(2)}, u32[]{:S(2)}) collective-permute-start(bf16[2,768,256]{2,1,0:T(8,128)(2,1)S(1)} %get-tuple-element.41), channel_id=1, source_target_pairs={{0,8},{1,9},{2,10},{3,11},{4,12},{5,13},{6,14},{7,15},{8,0},{9,1},... | collective-permute-start | bytes 2359304 | tf_op jit(solution)/shard_map/ppermute | solution.py:462
  437.6 36.0 %collective-permute-start.13 = (bf16[2,768,256]{2,1,0:T(8,128)(2,1)S(1)}, bf16[2,768,256]{2,1,0:T(8,128)(2,1)S(1)}, u32[]{:S(2)}, u32[]{:S(2)}) collective-permute-start(bf16[2,768,256]{2,1,0:T(8,128)(2,1)S(1)} %get-tuple-element.41), channel_id=1, source_target_pairs={{0,9},{1,8},{2,11},{3,10},{4,13},{5,12},{6,15},{7,14},{8,1},{9,0},... | collective-permute-start | bytes 2359304 | tf_op jit(solution)/shard_map/ppermute | solution.py:462
  439.0 34.6 %collective-permute-start.12 = (bf16[2,768,256]{2,1,0:T(8,128)(2,1)S(1)}, bf16[2,768,256]{2,1,0:T(8,128)(2,1)S(1)}, u32[]{:S(2)}, u32[]{:S(2)}) collective-permute-start(bf16[2,768,256]{2,1,0:T(8,128)(2,1)S(1)} %get-tuple-element.42.own), channel_id=1, source_target_pairs={{0,1},{1,0},{2,3},{3,2},{4,5},{5,4},{6,7},{7,6},{8,9},{9,8},{10,11... | collective-permute-start | bytes 2359304 | tf_op jit(solution)/shard_map/ppermute | solution.py:462
  (23 other events, 170.2 us)
Sparse Core Ops, SparseCore 0:
  10.1 44.6 all-gather.12
  57.0 50.1 all-gather.14
  161.1 34.3 all-gather.16
  208.0 59.4 all-gather.18
  269.0 62.1 all-gather.22
  347.9 37.8 all-gather.20
